TPU v7x, 512 devices: a whole 4x4x16 slice. The times are simulated.
512 devices in a mesh: dom: 128 (over z, x, core), rep: 4 (over y).
Axes of the slice: x: 4, y: 4, z: 16, core: 2. Of those that a mesh axis runs over, the one named last changes fastest.
Arguments:
- start_block: float32 [65536, 512], P(('dom', 'rep')), may hold values from -250 to 250
- restriction_maps: float32 [8, 8, 393216], P(None, None, ('dom', 'rep')), may hold values from -2 to 2
- send_rows: int32 [512, 64], P(('dom', 'rep')), may hold values from 0 to 767, as said below
- partner: int32 [393216], P(('dom', 'rep')), may hold values from 0 to 831, as said below
Outputs:
- basis: float32 [65536, 512], P(('dom', 'rep'))
- triangle: float32 [64, 64], replicated
Inputs may be any that keep to these rules, and one draw needn't show every extreme that they name: `send_rows`: row p holds four groups of 16 slots, for ends sent to the partitions at dom index d + 1, d - 1 and rep index r + 1, r - 1 (cyclic in rep). Group k holds distinct local edge-end indices of p in its first c slots, c even and at most 16, and 0 in the rest; c is the same for a link seen from both sides. Partitions at the two ends of dom send nothing outward. In every draw some dom link and some rep link carry exactly 16 ends. `partner`: the pairing is mutual: a value below 768 names a local end whose entry names this end back; the end in slot s of group k of send_rows has the value 128 * 6 + o * 16 + s with o = 1, 0, 3, 2 for k = 0, 1, 2, 3, and the neighbour's end in slot s of its group o has the corresponding value pointing back.
All inputs are finite; a program needn't handle non-finite values.
Results may differ from a plain program's by a relative error of at most 0.0003.
Values sent between devices are 32-bit elements; how exact they have to be, the bound alone decides.
A program may use at most 64 MiB of HBM per device.

v0:
```python
import math

import jax
import jax.numpy as jnp
from jax import lax
from jax.sharding import PartitionSpec as P

STALK = 8
COLS = 64


highest = lax.Precision.HIGHEST
filter_center = 21.0
filter_radius = 15.0


def passed_along(shard, axis, by):
    peers = lax.axis_size(axis)
    pairs = [(i, i + by) for i in range(peers) if 0 <= i + by < peers]
    return lax.ppermute(shard, axis, pairs)


def shifted(value, axis, steps):
    count = lax.axis_size(axis)
    pairs = [(source, (source + steps) % count) for source in range(count)]
    return lax.ppermute(value, axis, pairs)


def upper_cholesky(gram_matrix):
    return jnp.linalg.cholesky(gram_matrix).T


def lower_inverse(lower_factor):
    identity = jnp.eye(lower_factor.shape[0], dtype=lower_factor.dtype)
    return jax.scipy.linalg.solve_triangular(lower_factor, identity, lower=True)


def local(start_block, restriction_maps, send_rows, partner):
    node_count = start_block.shape[0]
    end_count = restriction_maps.shape[2]
    degree = end_count // node_count
    slot_count = send_rows.shape[1] // 4
    maps_four = restriction_maps.reshape(STALK, STALK, node_count, degree)
    send_index = send_rows[0]

    def laplace(values):
        stalks = values.reshape(node_count, STALK, COLS)
        own_proj = jnp.einsum("abnk,nbc->nkac", maps_four, stalks, precision=highest).reshape(
            end_count, STALK * COLS
        )
        outgoing = own_proj[send_index].reshape(4, slot_count, STALK * COLS)
        from_below = passed_along(outgoing[0], "dom", 1)
        from_above = passed_along(outgoing[1], "dom", -1)
        from_left = shifted(outgoing[2], "rep", 1)
        from_right = shifted(outgoing[3], "rep", -1)
        extended = jnp.concatenate([own_proj, from_below, from_above, from_left, from_right], 0)
        partner_proj = extended[partner]
        difference = (own_proj - partner_proj).reshape(node_count, degree, STALK, COLS)
        result = jnp.einsum("abnk,nkac->nbc", maps_four, difference, precision=highest)
        return result.reshape(node_count, STALK * COLS)

    first_term = (laplace(start_block) - filter_center * start_block) / filter_radius
    filtered = (
        2.0 * (laplace(first_term) - filter_center * first_term) / filter_radius - start_block
    )
    flat_rows = filtered.reshape(node_count * STALK, COLS)
    local_gram = jnp.einsum("rc,rd->cd", flat_rows, flat_rows, precision=highest)
    gram_sum = lax.psum(local_gram, ("dom", "rep"))
    upper_factor = upper_cholesky(gram_sum)
    inverse_lower = lower_inverse(upper_factor.T)
    solved = jnp.dot(flat_rows, inverse_lower.T, precision=highest)
    scaling = math.sqrt(node_count * STALK * lax.axis_size("dom") * lax.axis_size("rep"))
    return ((solved * scaling).reshape(node_count, STALK * COLS), upper_factor / scaling)


def solution(mesh):
    in_specs = (
        P(("dom", "rep"), None),
        P(None, None, ("dom", "rep")),
        P(("dom", "rep"), None),
        P(("dom", "rep")),
    )
    out_specs = (P(("dom", "rep"), None), P())
    return jax.shard_map(local, mesh=mesh, in_specs=in_specs, out_specs=out_specs, check_vma=False)
```

profile of v0, /device:TPU:1, one launch (start us, length us, event | category | flops | bytes accessed | tf_op | source)
XLA Modules:
  0.0 246.3 jit_solution(16984243248859289180)
XLA Ops:
  3.4 6.6 %reshape.92 = f32[8,8,128,6]{3,2,1,0:T(8,128)} reshape(f32[8,8,768]{2,1,0:T(8,128)} %param.5) | data formatting | bytes 393216 | tf_op jit(solution)/shard_map/reshape | solution.py:43
  10.0 10.0 %copy.15 = f32[8,8,128,6]{1,0,3,2:T(8,128)} copy(f32[8,8,128,6]{3,2,1,0:T(8,128)} %reshape.92) | data formatting | bytes 393216 | tf_op jit(solution)/shard_map/reshape | solution.py:43
  20.1 4.9 %convolution_bitcast_fusion.1 = f32[128,6,8,64]{3,2,1,0:T(8,128)S(1)} fusion(f32[128,8,64,1]{2,1,3,0:T(8,128)} %copy.29, f32[8,8,128,6]{1,0,3,2:T(8,128)} %copy.15), kind=kOutput, calls=%fused_computation.9 | convolution fusion | flops 37748736 | bytes 2031616 | tf_op jit(solution)/shard_map/abnk,nbc->nkac/dot_general | solution.py:48
  24.9 2.2 reshape.93
  27.1 2.1 gather_fusion
  29.2 5.5 %collective-permute-start.3 = (f32[16,512]{1,0:T(8,128)S(1)}, f32[16,512]{1,0:T(8,128)S(1)}, u32[]{:S(2)}, u32[]{:S(2)}) collective-permute-start(f32[16,512]{1,0:T(8,128)S(1)} %get-tuple-element.10), channel_id=1, source_target_pairs={{0,3},{1,0},{2,1},{3,2},{4,7},{5,4},{6,5},{7,6},{8,11},{9,8},{10,9... | collective-permute-start | bytes 98312 | tf_op jit(solution)/shard_map/ppermute | solution.py:26
  36.7 7.2 %collective-permute-start.1 = (f32[16,512]{1,0:T(8,128)S(1)}, f32[16,512]{1,0:T(8,128)S(1)}, u32[]{:S(2)}, u32[]{:S(2)}) collective-permute-start(f32[16,512]{1,0:T(8,128)S(1)} %get-tuple-element.12), channel_id=1, source_target_pairs={{4,0},{8,4},{12,8},{16,12},{20,16},{24,20},{28,24},{32,28},{36,32}... | collective-permute-start | bytes 98312 | tf_op jit(solution)/shard_map/ppermute | solution.py:20
  43.9 2.1 collective-permute-start
  47.6 10.0 %copy.16 = f32[8,8,128,6]{0,1,3,2:T(8,128)} copy(f32[8,8,128,6]{3,2,1,0:T(8,128)} %reshape.92) | data formatting | bytes 393216 | tf_op jit(solution)/shard_map/reshape | solution.py:43
  57.7 3.1 %gather_fusion.1 = f32[768,512]{1,0:T(8,128)} fusion(f32[832,512]{1,0:T(8,128)S(1)} %constant_dynamic-update-slice_fusion, s32[1024]{0:T(1024)S(1)} %pad_clamp_fusion), kind=kCustom, calls=%fused_computation.1 | custom fusion | bytes 3148800 | tf_op jit(solution)/shard_map/gather | solution.py:57
  60.8 3.5 %gather.18 = f32[128,6,8,64]{3,2,1,0:T(8,128)} reshape(f32[768,512]{1,0:T(8,128)} %gather_fusion.1) | data formatting | bytes 3145728 | tf_op jit(solution)/shard_map/gather | solution.py:57
  64.3 8.1 %fusion.4 = f32[128,8,64]{2,1,0:T(8,128)} fusion(f32[8,8,128,6]{0,1,3,2:T(8,128)S(1)} %copy-done, f32[128,6,8,64]{3,2,1,0:T(8,128)} %copy-done.2, f32[128,6,8,64]{3,2,1,0:T(8,128)} %gather.18), kind=kOutput, calls=%fused_computation.10 | convolution fusion | flops 38141952 | bytes 3604480 | tf_op jit(solution)/shard_map/abnk,nkac->nbc/dot_general | solution.py:59
  75.4 4.9 %convolution_bitcast_fusion = f32[128,6,8,64]{3,2,1,0:T(8,128)S(1)} fusion(f32[128,8,64,1]{2,1,3,0:T(8,128)} %copy.31, f32[8,8,128,6]{1,0,3,2:T(8,128)} %copy.15), kind=kOutput, calls=%fused_computation.8 | convolution fusion | flops 37748736 | bytes 2031616 | tf_op jit(solution)/shard_map/abnk,nbc->nkac/dot_general | solution.py:48
  80.3 2.1 reshape.96
  82.4 2.1 gather_fusion.2
  88.0 2.9 %collective-permute-start.7 = (f32[16,512]{1,0:T(8,128)S(1)}, f32[16,512]{1,0:T(8,128)S(1)}, u32[]{:S(2)}, u32[]{:S(2)}) collective-permute-start(f32[16,512]{1,0:T(8,128)S(1)} %get-tuple-element.6), channel_id=1, source_target_pairs={{0,3},{1,0},{2,1},{3,2},{4,7},{5,4},{6,5},{7,6},{8,11},{9,8},{10,9... | collective-permute-start | bytes 98312 | tf_op jit(solution)/shard_map/ppermute | solution.py:26
  90.9 2.4 collective-permute-start.6
  93.3 3.2 %collective-permute-start.5 = (f32[16,512]{1,0:T(8,128)S(1)}, f32[16,512]{1,0:T(8,128)S(1)}, u32[]{:S(2)}, u32[]{:S(2)}) collective-permute-start(f32[16,512]{1,0:T(8,128)S(1)} %get-tuple-element.8), channel_id=1, source_target_pairs={{4,0},{8,4},{12,8},{16,12},{20,16},{24,20},{28,24},{32,28},{36,32}... | collective-permute-start | bytes 98312 | tf_op jit(solution)/shard_map/ppermute | solution.py:20
  98.6 3.1 %gather_fusion.3 = f32[768,512]{1,0:T(8,128)} fusion(f32[832,512]{1,0:T(8,128)S(1)} %constant_dynamic-update-slice_fusion.5, s32[1024]{0:T(1024)S(1)} %pad_clamp_fusion), kind=kCustom, calls=%fused_computation.3 | custom fusion | bytes 3148800 | tf_op jit(solution)/shard_map/gather | solution.py:57
  101.7 3.5 %gather.21 = f32[128,6,8,64]{3,2,1,0:T(8,128)} reshape(f32[768,512]{1,0:T(8,128)} %gather_fusion.3) | data formatting | bytes 3145728 | tf_op jit(solution)/shard_map/gather | solution.py:57
  105.2 8.1 %fusion.7 = f32[128,8,64]{2,1,0:T(8,128)} fusion(f32[8,8,128,6]{0,1,3,2:T(8,128)S(1)} %copy-done.1, f32[128,6,8,64]{3,2,1,0:T(8,128)} %copy-done.3, f32[128,6,8,64]{3,2,1,0:T(8,128)} %gather.21), kind=kOutput, calls=%fused_computation.11 | convolution fusion | flops 38141952 | bytes 3604480 | tf_op jit(solution)/shard_map/abnk,nkac->nbc/dot_general | solution.py:59
  116.9 114.5 %psum.7 = f32[64,64]{0,1:T(8,128)S(1)} all-reduce(f32[64,64]{0,1:T(8,128)S(1)} %fusion.19), channel_id=1, replica_groups=mesh['dom'=128,'rep'=4] {'dom','rep'}, use_global_device_ids=true, to_apply=%region_0.0 | all-reduce | flops 4096 | bytes 32768 | tf_op jit(solution)/shard_map/psum | solution.py:68
  231.5 5.8 %cholesky.17 = f32[64,64]{1,0:T(8,128)S(1)} custom-call(f32[64,64]{1,0:T(8,128)S(1)} %fusion.15), custom_call_target="Cholesky" | custom-call | tf_op jit(solution)/shard_map/jit(cholesky)/cholesky | solution.py:30
  239.4 4.9 %custom-call.7 = f32[1,64,64]{1,2,0:T(8,128)S(1)} custom-call(f32[1,64,64]{2,1,0:T(8,128)S(1)} %get-tuple-element.15), custom_call_target="InvertDiagBlocksLowerTriangular" | custom-call | tf_op jit(solution)/shard_map/jit(_solve_triangular)/triangular_solve | solution.py:35
  (58 shorter events, 22.3 us)
Async XLA Ops:
  24.9 2.2 copy-start.2
  29.2 18.3 %copy-start.5 = (s32[768]{0:T(1024)S(1)}, s32[768]{0:T(1024)}, u32[]{:S(2)}) copy-start(s32[768]{0:T(1024)} %param.7) | copy-start | bytes 9220
  29.2 28.4 %collective-permute-start.3 = (f32[16,512]{1,0:T(8,128)S(1)}, f32[16,512]{1,0:T(8,128)S(1)}, u32[]{:S(2)}, u32[]{:S(2)}) collective-permute-start(f32[16,512]{1,0:T(8,128)S(1)} %get-tuple-element.10), channel_id=1, source_target_pairs={{0,3},{1,0},{2,1},{3,2},{4,7},{5,4},{6,5},{7,6},{8,11},{9,8},{10,9... | collective-permute-start | bytes 98312 | tf_op jit(solution)/shard_map/ppermute | solution.py:26
  34.7 22.9 %collective-permute-start.2 = (f32[16,512]{1,0:T(8,128)S(1)}, f32[16,512]{1,0:T(8,128)S(1)}, u32[]{:S(2)}, u32[]{:S(2)}) collective-permute-start(f32[16,512]{1,0:T(8,128)S(1)} %get-tuple-element.11), channel_id=1, source_target_pairs={{0,1},{1,2},{2,3},{3,0},{4,5},{5,6},{6,7},{7,4},{8,9},{9,10},{10,1... | collective-permute-start | bytes 98312 | tf_op jit(solution)/shard_map/ppermute | solution.py:26
  36.7 21.0 %collective-permute-start.1 = (f32[16,512]{1,0:T(8,128)S(1)}, f32[16,512]{1,0:T(8,128)S(1)}, u32[]{:S(2)}, u32[]{:S(2)}) collective-permute-start(f32[16,512]{1,0:T(8,128)S(1)} %get-tuple-element.12), channel_id=1, source_target_pairs={{4,0},{8,4},{12,8},{16,12},{20,16},{24,20},{28,24},{32,28},{36,32}... | collective-permute-start | bytes 98312 | tf_op jit(solution)/shard_map/ppermute | solution.py:20
  43.9 13.7 %collective-permute-start = (f32[16,512]{1,0:T(8,128)S(1)}, f32[16,512]{1,0:T(8,128)S(1)}, u32[]{:S(2)}, u32[]{:S(2)}) collective-permute-start(f32[16,512]{1,0:T(8,128)S(1)} %get-tuple-element.13), channel_id=1, source_target_pairs={{0,4},{4,8},{8,12},{12,16},{16,20},{20,24},{24,28},{28,32},{32,36}... | collective-permute-start | bytes 98312 | tf_op jit(solution)/shard_map/ppermute | solution.py:20
  60.8 3.5 %copy-start = (f32[8,8,128,6]{0,1,3,2:T(8,128)S(1)}, f32[8,8,128,6]{0,1,3,2:T(8,128)}, u32[]{:S(2)}) copy-start(f32[8,8,128,6]{0,1,3,2:T(8,128)} %copy.16) | copy-start | bytes 589828
  73.7 0.7 copy-start.4
  80.3 2.1 copy-start.3
  84.6 12.0 %collective-permute-start.4 = (f32[16,512]{1,0:T(8,128)S(1)}, f32[16,512]{1,0:T(8,128)S(1)}, u32[]{:S(2)}, u32[]{:S(2)}) collective-permute-start(f32[16,512]{1,0:T(8,128)S(1)} %get-tuple-element.9), channel_id=1, source_target_pairs={{0,4},{4,8},{8,12},{12,16},{16,20},{20,24},{24,28},{28,32},{32,36}... | collective-permute-start | bytes 98312 | tf_op jit(solution)/shard_map/ppermute | solution.py:20
  88.0 10.6 %collective-permute-start.7 = (f32[16,512]{1,0:T(8,128)S(1)}, f32[16,512]{1,0:T(8,128)S(1)}, u32[]{:S(2)}, u32[]{:S(2)}) collective-permute-start(f32[16,512]{1,0:T(8,128)S(1)} %get-tuple-element.6), channel_id=1, source_target_pairs={{0,3},{1,0},{2,1},{3,2},{4,7},{5,4},{6,5},{7,6},{8,11},{9,8},{10,9... | collective-permute-start | bytes 98312 | tf_op jit(solution)/shard_map/ppermute | solution.py:26
  90.9 7.7 %collective-permute-start.6 = (f32[16,512]{1,0:T(8,128)S(1)}, f32[16,512]{1,0:T(8,128)S(1)}, u32[]{:S(2)}, u32[]{:S(2)}) collective-permute-start(f32[16,512]{1,0:T(8,128)S(1)} %get-tuple-element.7), channel_id=1, source_target_pairs={{0,1},{1,2},{2,3},{3,0},{4,5},{5,6},{6,7},{7,4},{8,9},{9,10},{10,1... | collective-permute-start | bytes 98312 | tf_op jit(solution)/shard_map/ppermute | solution.py:26
  93.3 5.2 %collective-permute-start.5 = (f32[16,512]{1,0:T(8,128)S(1)}, f32[16,512]{1,0:T(8,128)S(1)}, u32[]{:S(2)}, u32[]{:S(2)}) collective-permute-start(f32[16,512]{1,0:T(8,128)S(1)} %get-tuple-element.8), channel_id=1, source_target_pairs={{4,0},{8,4},{12,8},{16,12},{20,16},{24,20},{28,24},{32,28},{36,32}... | collective-permute-start | bytes 98312 | tf_op jit(solution)/shard_map/ppermute | solution.py:20
  101.7 3.5 %copy-start.1 = (f32[8,8,128,6]{0,1,3,2:T(8,128)S(1)}, f32[8,8,128,6]{0,1,3,2:T(8,128)}, u32[]{:S(2)}) copy-start(f32[8,8,128,6]{0,1,3,2:T(8,128)} %copy.16) | copy-start | bytes 589828
where the time goes:
time: 247 us; the launch traced here: 246 us
  blocking collectives  114 us (46%)
  local copies, waits for them, and re-layouts  59.9 us (24%)
  matrix products  27.9 us (11%)
  starting transfers between devices  27.1 us (11%)
  other arithmetic  13.8 us (6%)
    psum x1, blocking collectives, local(): gram_sum = lax.psum(local_gram, ('dom', 'rep'))  114 us
    reshape x3, local copies, waits for them, and re-layouts, local(): maps_four = restriction_maps.reshape(STALK, STALK, node_count, degree)  26.7 us
    dot_general x2, matrix products, laplace(): jnp.einsum('abnk,nkac->nbc', maps_four, difference, precision=highest)  16.2 us
    ppermute x4, starting transfers between devices, passed_along(): return lax.ppermute(shard, axis, pairs)  14.4 us
    gather x4, local copies, waits for them, and re-layouts, laplace(): partner_proj = extended[partner]  13.3 us
    ppermute x4, starting transfers between devices, shifted(): return lax.ppermute(value, axis, pairs)  12.7 us
    dot_general x2, matrix products, laplace(): jnp.einsum('abnk,nbc->nkac', maps_four, stalks, precision=highest)  9.72 us
    another operation x3, other arithmetic, upper_cholesky(): return jnp.linalg.cholesky(gram_matrix).T  6.52 us
  transfers between devices with their start and end apart: 8, of which 1 were waited for; matrix products, arithmetic and copies ran while one was open for 5% of the time, Pallas kernels for 0%

commit v1 on v0

v1 whole, which is shorter than its diff:
```python
import functools
import math

import jax
import jax.numpy as jnp
from jax import lax
from jax.experimental import pallas as pl
from jax.experimental.pallas import tpu as pltpu
from jax.sharding import PartitionSpec as P

MESH = pl.DeviceIdType.MESH
F32 = jnp.float32
BF16 = jnp.bfloat16

STALK = 8
COLS = 64
DEG = 6
NODE_DEV = 128
ENDS = NODE_DEV * DEG
BND = 16
SLOTS = 4 * BND
WIDE = STALK * COLS
PLANE_DOM = 8
CENTER = 21.0
RADIUS = 15.0


def split_two(x):
    hi = x.astype(BF16)
    lo = (x - hi.astype(F32)).astype(BF16)
    return hi, lo


def dot_nn(a, b):
    return lax.dot_general(a, b, (((1,), (0,)), ((), ())), preferred_element_type=F32)


def dot_nt(a, b):
    return lax.dot_general(a, b, (((1,), (1,)), ((), ())), preferred_element_type=F32)


def row_bcast(row):
    return jnp.broadcast_to(row, (8, row.shape[1]))


def drain(ref, count, sem):
    pltpu.make_async_copy(ref.at[pl.ds(0, count)], ref.at[pl.ds(0, count)], sem).wait()


def filter_kernel(
    n_dom,
    n_rep,
    send_ref,
    start_ref,
    maps_ref,
    partner_ref,
    f_ref,
    g_ref,
    rt_ref,
    rk_ref,
    coef_ref,
    ss_ref,
    vt_ref,
    vhl_ref,
    vx_ref,
    t_ref,
    rs_ref,
    ms_ref,
    vsend_ref,
    rrecv_ref,
    vrecv_ref,
    cpack_ref,
    gsl_ref,
    rsbuf_ref,
    zsend_ref,
    zbuf_ref,
    agbuf_ref,
    rsem,
    vsem,
    arsem,
):
    d = lax.axis_index("dom")
    r = lax.axis_index("rep")
    z_count = n_dom // PLANE_DOM
    plane = PLANE_DOM * n_rep
    z = d // PLANE_DOM
    base = z * PLANE_DOM
    q = (d - base) * n_rep + r

    def plane_peer(i):
        t = lax.rem(q + 1 + i, plane)
        return t, (base + t // n_rep, lax.rem(t, n_rep))

    def z_peer(i):
        t = lax.rem(z + 1 + i, z_count)
        return (t * PLANE_DOM + (d - base), r)

    up = lax.rem(d + 1, n_dom)
    down = lax.rem(d + n_dom - 1, n_dom)
    nxt = lax.rem(r + 1, n_rep)
    prv = lax.rem(r + n_rep - 1, n_rep)
    neighbours = ((up, r), (down, r), (d, nxt), (d, prv))

    barrier = pltpu.get_barrier_semaphore()
    for peer in neighbours:
        pl.semaphore_signal(barrier, inc=1, device_id=peer, device_id_type=MESH)

    def greet_plane(i, carry):
        pl.semaphore_signal(barrier, inc=1, device_id=plane_peer(i)[1], device_id_type=MESH)
        return carry

    def greet_z(i, carry):
        pl.semaphore_signal(barrier, inc=1, device_id=z_peer(i), device_id_type=MESH)
        return carry

    lax.fori_loop(0, z_count - 1, greet_z, 0)
    lax.fori_loop(0, plane - 1, greet_plane, 0)

    part = jnp.broadcast_to(partner_ref[...].astype(F32), (8, ENDS))
    end_id = lax.broadcasted_iota(jnp.int32, (8, ENDS), 1).astype(F32)
    node_id = jnp.floor((end_id + 0.5) * (1.0 / DEG))
    sub8 = lax.broadcasted_iota(jnp.int32, (8, ENDS), 0)
    extra = jnp.where(sub8 == 0, part, node_id)
    for t in range(DEG):
        cols = slice(t * 128, (t + 1) * 128)
        block = jnp.concatenate(
            [maps_ref[:, cols], extra[:, cols], jnp.zeros((56, 128), F32)], axis=0
        )
        rt_ref[cols, :] = block.T

    for t in range(4):
        vt_ref[t * 128 : (t + 1) * 128, :] = start_ref[:, t * 128 : (t + 1) * 128].T

    for s in range(SLOTS):
        rs_ref[s : s + 1, :] = rt_ref[pl.ds(send_ref[0, s], 1), :]
    rs = rs_ref[...]
    lane = lax.broadcasted_iota(jnp.int32, (SLOTS, 128), 1).astype(F32)
    slot = lax.broadcasted_iota(jnp.int32, (SLOTS, 1), 0)
    expect = (ENDS + jnp.bitwise_xor(slot, BND)).astype(F32)
    used = rs[:, 64:65] == expect
    hot = jnp.where(jnp.logical_and(rs[:, 65:66] == lane, used), 1.0, 0.0).astype(BF16)
    hot_wide = jnp.concatenate([hot, hot], axis=1)
    hot_tall = jnp.concatenate([hot, hot], axis=0)

    sub = lax.broadcasted_iota(jnp.int32, (128, 128), 0).astype(F32)
    rhl = []
    kk_rows = []
    for k in range(DEG):
        rk = rt_ref[pl.ds(k, NODE_DEV, stride=DEG), :].T
        rk_ref[k] = rk[0:64, :]
        p = rk[64:65, :]
        node = jnp.floor((p + 0.5) * (1.0 / DEG))
        kk_rows.append(p - DEG * node)
        one = jnp.where(sub == node, 1.0, 0.0).astype(BF16)
        ss_ref[0:128, k * 128 : (k + 1) * 128] = one
        ss_ref[128:256, k * 128 : (k + 1) * 128] = one
        hi, lo = split_two(rk[0:64, :])
        rhl.append(jnp.concatenate([hi, lo], axis=1))
    rhl = jnp.concatenate(rhl, axis=0)

    sub_b = lax.broadcasted_iota(jnp.int32, (8, 128), 0)
    own = [jnp.zeros((8, 128), F32) for _ in range(STALK)]
    for j in range(3):
        far = dot_nn(rhl, ss_ref[:, j * 256 : (j + 1) * 256])
        for h in range(2):
            k = 2 * j + h
            mate_map = far[0:64, h * 128 : (h + 1) * 128]
            for m in range(1, DEG):
                mate_map = jnp.where(
                    kk_rows[k] == float(m),
                    far[m * 64 : (m + 1) * 64, h * 128 : (h + 1) * 128],
                    mate_map,
                )
            for a2 in range(STALK):
                acc = jnp.zeros((8, 128), F32)
                for a in range(STALK):
                    coef = row_bcast(rk_ref[k, a * 8 + a2 : a * 8 + a2 + 1, :])
                    acc = acc + coef * mate_map[a * 8 : (a + 1) * 8, :]
                    own[a2] = own[a2] + coef * rk_ref[k, a * 8 : (a + 1) * 8, :]
                coef_ref[k, a2 * 8 : (a2 + 1) * 8, :] = acc * (-1.0 / RADIUS)
    for a2 in range(STALK):
        coef_ref[DEG, a2 * 8 : (a2 + 1) * 8, :] = (
            own[a2] - jnp.where(sub_b == a2, CENTER, 0.0)
        ) * (1.0 / RADIUS)

    def spread(values_ref):
        hi, lo = split_two(values_ref[...])
        vhl_ref[:, 0:128] = hi
        vhl_ref[:, 128:256] = lo

    def value_copies(step):
        return [
            pltpu.make_async_remote_copy(
                src_ref=vsend_ref.at[step, pl.ds(k * BND, BND), :],
                dst_ref=vrecv_ref.at[step, pl.ds((k ^ 1) * BND, BND), :],
                send_sem=vsem.at[0, step, k],
                recv_sem=vsem.at[1, step, k ^ 1],
                device_id=neighbours[k],
                device_id_type=MESH,
            )
            for k in range(4)
        ]

    map_copies = [
        pltpu.make_async_remote_copy(
            src_ref=rs_ref.at[pl.ds(k * BND, BND), :],
            dst_ref=rrecv_ref.at[pl.ds((k ^ 1) * BND, BND), :],
            send_sem=rsem.at[0, k],
            recv_sem=rsem.at[1, k ^ 1],
            device_id=neighbours[k],
            device_id_type=MESH,
        )
        for k in range(4)
    ]

    def recv_waits(copies):
        for copy in copies:
            copy.wait_recv()

    def outgoing(step):
        vsend_ref[step] = dot_nt(hot_wide, vhl_ref[...])

    def local_part(own_ref, out_ref, combine):
        for j in range(3):
            vx_ref[:, j * 256 : (j + 1) * 256] = dot_nn(
                vhl_ref[...], ss_ref[:, j * 256 : (j + 1) * 256]
            )

        def columns(i, carry):
            acc = [[jnp.zeros((8, 128), F32) for _ in range(2)] for _ in range(STALK)]
            for k in range(DEG + 1):
                for b in range(STALK):
                    vals = []
                    for h in range(2):
                        at = pl.ds(pl.multiple_of(b * COLS + i * 16 + h * 8, 8), 8)
                        if k == DEG:
                            vals.append(own_ref[at, :])
                        else:
                            vals.append(vx_ref[at, k * 128 : (k + 1) * 128])
                    for a2 in range(STALK):
                        coef = row_bcast(coef_ref[k, a2 * 8 + b : a2 * 8 + b + 1, :])
                        for h in range(2):
                            acc[a2][h] = acc[a2][h] + coef * vals[h]
            for a2 in range(STALK):
                for h in range(2):
                    at = pl.ds(pl.multiple_of(a2 * COLS + i * 16 + h * 8, 8), 8)
                    out_ref[at, :] = combine(acc[a2][h], at)
            return carry

        lax.fori_loop(0, 4, columns, 0)

    def remote_part(step):
        low = lax.broadcasted_iota(jnp.int32, (8, 128), 1) < SLOTS
        turned = []
        for t in range(4):
            block = vrecv_ref[step, :, t * 128 : (t + 1) * 128]
            turned.append(jnp.concatenate([block, block], axis=0).T)
        for cg in range(8):
            acc = [jnp.zeros((8, 128), F32) for _ in range(STALK)]
            for b in range(STALK):
                row = b * COLS + cg * 8
                val = turned[row // 128][row % 128 : row % 128 + 8, :]
                for a2 in range(STALK):
                    coef = row_bcast(ms_ref[a2 * 8 + b : a2 * 8 + b + 1, :])
                    acc[a2] = acc[a2] + coef * val
            for a2 in range(STALK):
                hi = acc[a2].astype(BF16).astype(F32)
                cpack_ref[a2 * COLS + cg * 8 : a2 * COLS + cg * 8 + 8, :] = jnp.where(
                    low, hi, acc[a2] - hi
                )
        return dot_nn(cpack_ref[...].astype(BF16), hot_tall)

    spread(vt_ref)
    outgoing(0)
    pl.semaphore_wait(barrier, 4 + (plane - 1) + (z_count - 1))
    for copy in map_copies:
        copy.start()
    first_copies = value_copies(0)
    for copy in first_copies:
        copy.start()
    local_part(vt_ref, t_ref, lambda acc, at: acc)

    recv_waits(map_copies)
    far_maps = jnp.concatenate([rrecv_ref[...], rrecv_ref[...]], axis=0).T
    own_maps = jnp.concatenate([rs, rs], axis=0).T
    for a2 in range(STALK):
        acc = jnp.zeros((8, 128), F32)
        for a in range(STALK):
            acc = acc + row_bcast(own_maps[a * 8 + a2 : a * 8 + a2 + 1, :]) * (
                far_maps[a * 8 : (a + 1) * 8, :]
            )
        ms_ref[a2 * 8 : (a2 + 1) * 8, :] = acc * (-1.0 / RADIUS)
    recv_waits(first_copies)
    t_ref[...] = t_ref[...] + remote_part(0)

    spread(t_ref)
    outgoing(1)
    second_copies = value_copies(1)
    for copy in second_copies:
        copy.start()
    local_part(t_ref, vt_ref, lambda acc, at: 2.0 * acc - vt_ref[at, :])
    recv_waits(second_copies)
    vt_ref[...] = vt_ref[...] + 2.0 * remote_part(1)

    spread(vt_ref)
    tall = jnp.concatenate(
        [
            jnp.concatenate(
                [vhl_ref[a * COLS : (a + 1) * COLS, h * 128 : (h + 1) * 128] for a in range(STALK)],
                axis=1,
            )
            for h in range(2)
        ],
        axis=0,
    )
    prod = dot_nt(tall, tall)
    half = prod[0:64, :] + prod[64:128, :]
    both = half + pltpu.roll(half, 64, 1)
    lane32 = lax.broadcasted_iota(jnp.int32, (32, 128), 1)
    packed = jnp.where(lane32 < 64, both[0:32, :], both[32:64, :])
    for i in range(plane):
        gsl_ref[i] = packed[i : i + 1, :]

    def reduce_start(i, carry):
        t, peer = plane_peer(i)
        pltpu.make_async_remote_copy(
            src_ref=gsl_ref.at[t],
            dst_ref=rsbuf_ref.at[q],
            send_sem=arsem.at[0],
            recv_sem=arsem.at[1],
            device_id=peer,
            device_id_type=MESH,
        ).start()
        return carry

    lax.fori_loop(0, plane - 1, reduce_start, 0)
    rsbuf_ref[q] = gsl_ref[q]
    for t in range(4):
        f_ref[:, t * 128 : (t + 1) * 128] = vt_ref[t * 128 : (t + 1) * 128, :].T
    drain(rsbuf_ref, plane - 1, arsem.at[1])

    def total(ref, count):
        rows = [ref[i] for i in range(count)]
        while len(rows) > 1:
            rows = [rows[i] + rows[i + 1] for i in range(0, len(rows) - 1, 2)] + (
                [rows[-1]] if len(rows) % 2 else []
            )
        return rows[0]

    part_sum = total(rsbuf_ref, plane)
    zsend_ref[0] = part_sum

    def z_start(i, carry):
        pltpu.make_async_remote_copy(
            src_ref=zsend_ref.at[0],
            dst_ref=zbuf_ref.at[z],
            send_sem=arsem.at[2],
            recv_sem=arsem.at[3],
            device_id=z_peer(i),
            device_id_type=MESH,
        ).start()
        return carry

    lax.fori_loop(0, z_count - 1, z_start, 0)
    zbuf_ref[z] = part_sum
    drain(zbuf_ref, z_count - 1, arsem.at[3])
    slice_sum = total(zbuf_ref, z_count)
    zsend_ref[1] = slice_sum

    def gather_start(i, carry):
        pltpu.make_async_remote_copy(
            src_ref=zsend_ref.at[1],
            dst_ref=agbuf_ref.at[q],
            send_sem=arsem.at[4],
            recv_sem=arsem.at[5],
            device_id=plane_peer(i)[1],
            device_id_type=MESH,
        ).start()
        return carry

    lax.fori_loop(0, plane - 1, gather_start, 0)
    agbuf_ref[q] = slice_sum
    drain(agbuf_ref, plane - 1, arsem.at[5])
    for i in range(plane):
        g_ref[i : i + 1, :] = agbuf_ref[i]

    for copies in (map_copies, first_copies, second_copies):
        for copy in copies:
            copy.wait_send()
    drain(rsbuf_ref, plane - 1, arsem.at[0])
    drain(zbuf_ref, z_count - 1, arsem.at[2])
    drain(agbuf_ref, plane - 1, arsem.at[4])


def solve_kernel(scaling, f_ref, g_ref, basis_ref, triangle_ref):
    g = g_ref[...]
    turned = pltpu.roll(g, 64, 1)
    lane32 = lax.broadcasted_iota(jnp.int32, (32, 128), 1)
    row32 = lax.broadcasted_iota(jnp.int32, (32, 128), 0)
    top = jnp.where(lane32 < 64, g, jnp.where(lane32 - 64 == row32, 1.0, 0.0))
    bottom = jnp.where(lane32 < 64, turned, jnp.where(lane32 - 96 == row32, 1.0, 0.0))
    work = [top[i * 8 : (i + 1) * 8, :] for i in range(4)] + [
        bottom[i * 8 : (i + 1) * 8, :] for i in range(4)
    ]
    sub = lax.broadcasted_iota(jnp.int32, (8, 128), 0)
    for k in range(COLS):
        group, row = k // 8, k % 8
        pivot_row = work[group][row : row + 1, :]
        scaled = pivot_row / pivot_row[:, k : k + 1]
        for i in range(group, 8):
            col = work[i][:, k : k + 1]
            update = col * scaled
            if i == group:
                update = jnp.where(sub > row, update, 0.0)
            work[i] = work[i] - update
    lane = lax.broadcasted_iota(jnp.int32, (8, 128), 1)
    rows_out = []
    for i in range(8):
        diag = jnp.sum(jnp.where(lane == sub + 8 * i, work[i], 0.0), axis=1, keepdims=True)
        rows_out.append(work[i] / jnp.sqrt(diag))
    full = jnp.concatenate(rows_out, axis=0)
    lane64 = lax.broadcasted_iota(jnp.int32, (COLS, 128), 1)
    row64 = lax.broadcasted_iota(jnp.int32, (COLS, 128), 0)
    triangle_ref[...] = jnp.where(lane64 >= row64, full * (1.0 / scaling), 0.0)[:, 0:COLS]
    full = full * scaling
    block = jnp.concatenate(
        [
            jnp.where(lane64 < 64, pltpu.roll(full, 64, 1), 0.0),
            jnp.where(lane64 < 64, 0.0, full),
        ],
        axis=0,
    )
    bhi, blo = split_two(block)
    right = jnp.concatenate([bhi, bhi, blo], axis=1)
    for t in range(4):
        fhi, flo = split_two(f_ref[:, t * 128 : (t + 1) * 128])
        left = jnp.concatenate([fhi, flo, fhi], axis=1)
        basis_ref[:, t * 128 : (t + 1) * 128] = dot_nt(left, right)


def local(n_dom, n_rep, start_block, restriction_maps, send_rows, partner):
    z_count = n_dom // PLANE_DOM
    plane = PLANE_DOM * n_rep
    vmem = pl.BlockSpec(memory_space=pltpu.VMEM)
    smem = pl.BlockSpec(memory_space=pltpu.SMEM)
    maps = restriction_maps.reshape(STALK * STALK, ENDS)
    partner = partner.reshape(1, ENDS)
    f_rows, gram = pl.pallas_call(
        functools.partial(filter_kernel, n_dom, n_rep),
        out_shape=[
            jax.ShapeDtypeStruct((NODE_DEV, WIDE), F32),
            jax.ShapeDtypeStruct((32, 128), F32),
        ],
        in_specs=[smem, vmem, vmem, vmem],
        out_specs=[vmem, vmem],
        scratch_shapes=[
            pltpu.VMEM((ENDS, 128), F32),
            pltpu.VMEM((DEG, 64, 128), F32),
            pltpu.VMEM((DEG + 1, 64, 128), F32),
            pltpu.VMEM((256, ENDS), BF16),
            pltpu.VMEM((WIDE, 128), F32),
            pltpu.VMEM((WIDE, 256), BF16),
            pltpu.VMEM((WIDE, ENDS), F32),
            pltpu.VMEM((WIDE, 128), F32),
            pltpu.VMEM((SLOTS, 128), F32),
            pltpu.VMEM((64, 128), F32),
            pltpu.VMEM((2, SLOTS, WIDE), F32),
            pltpu.VMEM((SLOTS, 128), F32),
            pltpu.VMEM((2, SLOTS, WIDE), F32),
            pltpu.VMEM((WIDE, 128), F32),
            pltpu.VMEM((plane, 1, 128), F32),
            pltpu.VMEM((plane, 1, 128), F32),
            pltpu.VMEM((2, 1, 128), F32),
            pltpu.VMEM((z_count, 1, 128), F32),
            pltpu.VMEM((plane, 1, 128), F32),
            pltpu.SemaphoreType.DMA((2, 4)),
            pltpu.SemaphoreType.DMA((2, 2, 4)),
            pltpu.SemaphoreType.DMA((6,)),
        ],
        compiler_params=pltpu.CompilerParams(
            collective_id=0, has_side_effects=True, vmem_limit_bytes=40 * 1024 * 1024
        ),
        name="filter_and_gram",
    )(send_rows, start_block, maps, partner)
    scaling = math.sqrt(NODE_DEV * STALK * n_dom * n_rep)
    return pl.pallas_call(
        functools.partial(solve_kernel, scaling),
        out_shape=[
            jax.ShapeDtypeStruct((NODE_DEV, WIDE), F32),
            jax.ShapeDtypeStruct((COLS, COLS), F32),
        ],
        in_specs=[vmem, vmem],
        out_specs=[vmem, vmem],
        compiler_params=pltpu.CompilerParams(vmem_limit_bytes=16 * 1024 * 1024),
        name="factor_and_solve",
    )(f_rows, gram)


def solution(mesh):
    n_dom, n_rep = mesh.shape["dom"], mesh.shape["rep"]
    in_specs = (
        P(("dom", "rep"), None),
        P(None, None, ("dom", "rep")),
        P(("dom", "rep"), None),
        P(("dom", "rep")),
    )
    out_specs = (P(("dom", "rep"), None), P())
    return jax.shard_map(
        functools.partial(local, n_dom, n_rep),
        mesh=mesh,
        in_specs=in_specs,
        out_specs=out_specs,
        check_vma=False,
    )
```

time: 247 us -> 53.3 us (0.22)
  blocking collectives: 114 us -> 0 us
  local copies, waits for them, and re-layouts: 59.9 us -> 2.58 us
  Pallas kernels: 0 us -> 49.9 us
  matrix products: 27.9 us -> 0 us
  starting transfers between devices: 27.1 us -> 0 us
  other arithmetic: 13.8 us -> 0 us
    psum x1 -> x0, blocking collectives: 114 us -> none  [local(): gram_sum = lax.psum(local_gram, ('dom', 'rep'))]
    pallas_call x0 -> x2, Pallas kernels: none -> 49.9 us  [the longest x1 43.5 us: local(): pl.pallas_call(functools.partial(filter_kernel, n_dom, n_rep), out_shape=...]
    reshape x9 -> x1, local copies, waits for them, and re-layouts: 34 us -> 0.7 us  [local(): partner = partner.reshape(1, ENDS)]
    dot_general x6 -> x0, matrix products: 27.7 us -> none  [the longest x2 16.2 us: laplace(): jnp.einsum('abnk,nkac->nbc', maps_four, difference, precision=highest)]
    ppermute x8 -> x0, starting transfers between devices: 27.1 us -> none  [the longest x4 14.4 us: passed_along(): return lax.ppermute(shard, axis, pairs)]
    gather x6 -> x0, local copies, waits for them, and re-layouts: 17.5 us -> none  [the longest x4 13.3 us: laplace(): partner_proj = extended[partner]]
    another operation x4 -> x0, other arithmetic: 11.4 us -> none  [the longest x3 6.52 us: upper_cholesky(): return jnp.linalg.cholesky(gram_matrix).T]
    unnamed x22 -> x6, local copies, waits for them, and re-layouts: 5.52 us -> 1.88 us
  transfers between devices with their start and end apart: 8 -> 0, of which waited for: 1 -> 0; matrix products, arithmetic and copies ran while one was open for 5% -> 0% of each run, Pallas kernels for 0% -> 0%
where the time goes in v1:
time: 53.3 us; the launch traced here: 53.1 us
  Pallas kernels  49.9 us (94%)
  local copies, waits for them, and re-layouts  2.58 us (5%)
  between operations  0.65 us (1%)
    pallas_call x1, Pallas kernels, local(): pl.pallas_call(functools.partial(filter_kernel, n_dom, n_rep), out_shape=...  43.5 us
    pallas_call x1, Pallas kernels, local(): pl.pallas_call(functools.partial(solve_kernel, scaling), out_shape=[jax.S...  6.44 us
    unnamed x6, local copies, waits for them, and re-layouts  1.88 us

profile of v1, /device:TPU:1, one launch (start us, length us, event | category | flops | bytes accessed | tf_op | source)
XLA Modules:
  0.0 53.1 jit_solution(3440176395510892878)
XLA Ops:
  0.6 0.0 copy-start.2
  0.6 0.7 %reshape.11.partner_ref = s32[1,768]{1,0:T(1,128)S(1)} reshape(s32[768]{0:T(1024)} %param.7) | data formatting | bytes 6144 | tf_op jit(solution)/shard_map/reshape | solution.py:447
  1.3 0.0 copy-done.2
  1.3 0.0 copy-start
  1.3 0.9 %copy-done = f32[128,512]{1,0:T(8,128)S(1)} copy-done((f32[128,512]{1,0:T(8,128)S(1)}, f32[128,512]{1,0:T(8,128)}, u32[]{:S(2)}) %copy-start) | copy-done | bytes 262168
  2.3 0.0 copy-start.1
  2.3 0.9 %copy-done.1 = f32[8,8,768]{2,1,0:T(8,128)S(1)} copy-done((f32[8,8,768]{2,1,0:T(8,128)S(1)}, f32[8,8,768]{2,1,0:T(8,128)}, u32[]{:S(2)}) %copy-start.1) | copy-done | bytes 196632
  3.2 43.5 %filter_and_gram.1 = (f32[128,512]{1,0:T(8,128)S(1)}, f32[32,128]{1,0:T(8,128)S(1)}) custom-call(s32[1,64]{1,0:T(1,128)S(1)} %copy-done.2, f32[128,512]{1,0:T(8,128)S(1)} %copy-done, f32[64,768]{1,0:T(8,128)S(1)} %bitcast.1, s32[1,768]{1,0:T(1,128)S(1)} %reshape.11.partner_ref), custom_call_target="tpu_custom_call" | custom-call | tf_op jit(solution)/shard_map/filter_and_gram/pallas_call | solution.py:448
  46.7 6.4 %factor_and_solve.1 = (f32[128,512]{1,0:T(8,128)}, f32[64,64]{1,0:T(8,128)}) custom-call(f32[128,512]{1,0:T(8,128)S(1)} %get-tuple-element.4.f_ref, f32[32,128]{1,0:T(8,128)S(1)} %get-tuple-element.5.g_ref), custom_call_target="tpu_custom_call" | custom-call | tf_op jit(solution)/shard_map/factor_and_solve/pallas_call | solution.py:486
Async XLA Ops:
  0.6 0.7 %copy-start.2 = (s32[1,64]{1,0:T(1,128)S(1)}, s32[1,64]{1,0:T(1,128)}, u32[]{:S(2)}) copy-start(s32[1,64]{1,0:T(1,128)} %send_ref.1) | copy-start | bytes 772
  1.3 1.0 %copy-start = (f32[128,512]{1,0:T(8,128)S(1)}, f32[128,512]{1,0:T(8,128)}, u32[]{:S(2)}) copy-start(f32[128,512]{1,0:T(8,128)} %start_ref.1) | copy-start | bytes 786436
  2.3 0.9 %copy-start.1 = (f32[8,8,768]{2,1,0:T(8,128)S(1)}, f32[8,8,768]{2,1,0:T(8,128)}, u32[]{:S(2)}) copy-start(f32[8,8,768]{2,1,0:T(8,128)} %param.5) | copy-start | bytes 589828

commit v2 on v1

--- a/solution.py
+++ b/solution.py
@@ -50,12 +50,16 @@
 def filter_kernel(
     n_dom,
     n_rep,
-    send_ref,
+    start_hbm,
+    maps_hbm,
+    send_hbm,
+    partner_hbm,
+    f_ref,
+    g_ref,
     start_ref,
     maps_ref,
+    send_ref,
     partner_ref,
-    f_ref,
-    g_ref,
     rt_ref,
     rk_ref,
     coef_ref,
@@ -78,6 +82,9 @@
     rsem,
     vsem,
     arsem,
+    insem,
+    xsem,
+    zsem,
 ):
     d = lax.axis_index("dom")
     r = lax.axis_index("rep")
@@ -101,22 +108,46 @@
     prv = lax.rem(r + n_rep - 1, n_rep)
     neighbours = ((up, r), (down, r), (d, nxt), (d, prv))
 
+    loads = [
+        pltpu.make_async_copy(src, dst, insem.at[i])
+        for i, (src, dst) in enumerate(
+            (
+                (send_hbm, send_ref),
+                (start_hbm, start_ref),
+                (maps_hbm, maps_ref),
+                (partner_hbm, partner_ref),
+            )
+        )
+    ]
+    for load in loads:
+        load.start()
+
+    mine = d - base
+    other_core = d + 1 - 2 * lax.rem(d, 2)
+    x_peers = [(base + lax.rem(mine + 2 * i, PLANE_DOM), r) for i in range(1, PLANE_DOM // 2)]
+    near = [(up, r), (down, r)]
+    near += [(base + lax.rem(mine + i, PLANE_DOM), r) for i in range(1, PLANE_DOM)]
+    for i in range(1, n_rep):
+        turn = lax.rem(r + i, n_rep)
+        near += [(d, turn), (other_core, turn)]
+
+    def z_shift(by):
+        return (lax.rem(z + z_count + by, z_count) * PLANE_DOM + mine, r)
+
+    near += [z_shift(by) for by in (1, -1, 2, -2)]
     barrier = pltpu.get_barrier_semaphore()
-    for peer in neighbours:
+    for peer in near:
         pl.semaphore_signal(barrier, inc=1, device_id=peer, device_id_type=MESH)
 
-    def greet_plane(i, carry):
-        pl.semaphore_signal(barrier, inc=1, device_id=plane_peer(i)[1], device_id_type=MESH)
-        return carry
-
-    def greet_z(i, carry):
-        pl.semaphore_signal(barrier, inc=1, device_id=z_peer(i), device_id_type=MESH)
-        return carry
-
-    lax.fori_loop(0, z_count - 1, greet_z, 0)
-    lax.fori_loop(0, plane - 1, greet_plane, 0)
-
-    part = jnp.broadcast_to(partner_ref[...].astype(F32), (8, ENDS))
+    loads[0].wait()
+    loads[1].wait()
+    for s in range(SLOTS):
+        node = lax.div(send_ref[0, s], DEG)
+        vsend_ref[0, s : s + 1, :] = start_ref[pl.ds(node, 1), :]
+    loads[2].wait()
+    loads[3].wait()
+
+    part = jnp.broadcast_to(partner_ref[...].reshape(1, ENDS).astype(F32), (8, ENDS))
     end_id = lax.broadcasted_iota(jnp.int32, (8, ENDS), 1).astype(F32)
     node_id = jnp.floor((end_id + 0.5) * (1.0 / DEG))
     sub8 = lax.broadcasted_iota(jnp.int32, (8, ENDS), 0)
@@ -124,7 +155,7 @@
     for t in range(DEG):
         cols = slice(t * 128, (t + 1) * 128)
         block = jnp.concatenate(
-            [maps_ref[:, cols], extra[:, cols], jnp.zeros((56, 128), F32)], axis=0
+            [maps_ref[:, :, cols].reshape(64, 128), extra[:, cols], jnp.zeros((56, 128), F32)], axis=0
         )
         rt_ref[cols, :] = block.T
 
@@ -157,6 +188,40 @@
         hi, lo = split_two(rk[0:64, :])
         rhl.append(jnp.concatenate([hi, lo], axis=1))
     rhl = jnp.concatenate(rhl, axis=0)
+
+    def value_copies(step):
+        return [
+            pltpu.make_async_remote_copy(
+                src_ref=vsend_ref.at[step, pl.ds(k * BND, BND), :],
+                dst_ref=vrecv_ref.at[step, pl.ds((k ^ 1) * BND, BND), :],
+                send_sem=vsem.at[0, step, k],
+                recv_sem=vsem.at[1, step, k ^ 1],
+                device_id=neighbours[k],
+                device_id_type=MESH,
+            )
+            for k in range(4)
+        ]
+
+    map_copies = [
+        pltpu.make_async_remote_copy(
+            src_ref=rs_ref.at[pl.ds(k * BND, BND), :],
+            dst_ref=rrecv_ref.at[pl.ds((k ^ 1) * BND, BND), :],
+            send_sem=rsem.at[0, k],
+            recv_sem=rsem.at[1, k ^ 1],
+            device_id=neighbours[k],
+            device_id_type=MESH,
+        )
+        for k in range(4)
+    ]
+
+    pl.semaphore_wait(barrier, len(near))
+    first_copies = value_copies(0)
+    for copy in first_copies + map_copies:
+        copy.start()
+    for peer in x_peers:
+        pl.semaphore_signal(xsem, inc=1, device_id=peer, device_id_type=MESH)
+    for by in (2, -2):
+        pl.semaphore_signal(zsem.at[0], inc=1, device_id=z_shift(by), device_id_type=MESH)
 
     sub_b = lax.broadcasted_iota(jnp.int32, (8, 128), 0)
     own = [jnp.zeros((8, 128), F32) for _ in range(STALK)]
@@ -188,31 +253,6 @@
         vhl_ref[:, 0:128] = hi
         vhl_ref[:, 128:256] = lo
 
-    def value_copies(step):
-        return [
-            pltpu.make_async_remote_copy(
-                src_ref=vsend_ref.at[step, pl.ds(k * BND, BND), :],
-                dst_ref=vrecv_ref.at[step, pl.ds((k ^ 1) * BND, BND), :],
-                send_sem=vsem.at[0, step, k],
-                recv_sem=vsem.at[1, step, k ^ 1],
-                device_id=neighbours[k],
-                device_id_type=MESH,
-            )
-            for k in range(4)
-        ]
-
-    map_copies = [
-        pltpu.make_async_remote_copy(
-            src_ref=rs_ref.at[pl.ds(k * BND, BND), :],
-            dst_ref=rrecv_ref.at[pl.ds((k ^ 1) * BND, BND), :],
-            send_sem=rsem.at[0, k],
-            recv_sem=rsem.at[1, k ^ 1],
-            device_id=neighbours[k],
-            device_id_type=MESH,
-        )
-        for k in range(4)
-    ]
-
     def recv_waits(copies):
         for copy in copies:
             copy.wait_recv()
@@ -271,13 +311,6 @@
         return dot_nn(cpack_ref[...].astype(BF16), hot_tall)
 
     spread(vt_ref)
-    outgoing(0)
-    pl.semaphore_wait(barrier, 4 + (plane - 1) + (z_count - 1))
-    for copy in map_copies:
-        copy.start()
-    first_copies = value_copies(0)
-    for copy in first_copies:
-        copy.start()
     local_part(vt_ref, t_ref, lambda acc, at: acc)
 
     recv_waits(map_copies)
@@ -298,6 +331,9 @@
     second_copies = value_copies(1)
     for copy in second_copies:
         copy.start()
+    pl.semaphore_wait(zsem.at[0], 2)
+    for by in (4, -4):
+        pl.semaphore_signal(zsem.at[1], inc=1, device_id=z_shift(by), device_id_type=MESH)
     local_part(t_ref, vt_ref, lambda acc, at: 2.0 * acc - vt_ref[at, :])
     recv_waits(second_copies)
     vt_ref[...] = vt_ref[...] + 2.0 * remote_part(1)
@@ -321,6 +357,8 @@
     for i in range(plane):
         gsl_ref[i] = packed[i : i + 1, :]
 
+    pl.semaphore_wait(xsem, len(x_peers))
+
     def reduce_start(i, carry):
         t, peer = plane_peer(i)
         pltpu.make_async_remote_copy(
@@ -349,6 +387,7 @@
 
     part_sum = total(rsbuf_ref, plane)
     zsend_ref[0] = part_sum
+    pl.semaphore_wait(zsem.at[1], 2)
 
     def z_start(i, carry):
         pltpu.make_async_remote_copy(
@@ -442,18 +481,24 @@
     z_count = n_dom // PLANE_DOM
     plane = PLANE_DOM * n_rep
     vmem = pl.BlockSpec(memory_space=pltpu.VMEM)
-    smem = pl.BlockSpec(memory_space=pltpu.SMEM)
-    maps = restriction_maps.reshape(STALK * STALK, ENDS)
-    partner = partner.reshape(1, ENDS)
+    hbm = pl.BlockSpec(memory_space=pltpu.HBM)
+    inputs = [
+        pltpu.with_memory_space_constraint(value, pltpu.HBM)
+        for value in (start_block, restriction_maps, send_rows, partner)
+    ]
     f_rows, gram = pl.pallas_call(
         functools.partial(filter_kernel, n_dom, n_rep),
         out_shape=[
-            jax.ShapeDtypeStruct((NODE_DEV, WIDE), F32),
-            jax.ShapeDtypeStruct((32, 128), F32),
+            pltpu.VMEM((NODE_DEV, WIDE), F32),
+            pltpu.VMEM((32, 128), F32),
         ],
-        in_specs=[smem, vmem, vmem, vmem],
+        in_specs=[hbm, hbm, hbm, hbm],
         out_specs=[vmem, vmem],
         scratch_shapes=[
+            pltpu.VMEM((NODE_DEV, WIDE), F32),
+            pltpu.VMEM((STALK, STALK, ENDS), F32),
+            pltpu.SMEM((1, SLOTS), jnp.int32),
+            pltpu.VMEM((ENDS,), jnp.int32),
             pltpu.VMEM((ENDS, 128), F32),
             pltpu.VMEM((DEG, 64, 128), F32),
             pltpu.VMEM((DEG + 1, 64, 128), F32),
@@ -476,12 +521,15 @@
             pltpu.SemaphoreType.DMA((2, 4)),
             pltpu.SemaphoreType.DMA((2, 2, 4)),
             pltpu.SemaphoreType.DMA((6,)),
+            pltpu.SemaphoreType.DMA((4,)),
+            pltpu.SemaphoreType.REGULAR,
+            pltpu.SemaphoreType.REGULAR((2,)),
         ],
         compiler_params=pltpu.CompilerParams(
             collective_id=0, has_side_effects=True, vmem_limit_bytes=40 * 1024 * 1024
         ),
         name="filter_and_gram",
-    )(send_rows, start_block, maps, partner)
+    )(*inputs)
     scaling = math.sqrt(NODE_DEV * STALK * n_dom * n_rep)
     return pl.pallas_call(
         functools.partial(solve_kernel, scaling),

time: 53.3 us -> 48 us (0.901)
  Pallas kernels: 49.9 us -> 47.2 us
  local copies, waits for them, and re-layouts: 2.58 us -> 0 us
    pallas_call x1, Pallas kernels: 43.5 us -> 40.8 us  [local(): pl.pallas_call(functools.partial(filter_kernel, n_dom, n_rep), out_shape=...]
    unnamed x6 -> x0, local copies, waits for them, and re-layouts: 1.88 us -> none
    reshape x1 -> x0, local copies, waits for them, and re-layouts: 0.7 us -> none  [local(): partner = partner.reshape(1, ENDS)]
where the time goes in v2:
time: 48 us; the launch traced here: 47.8 us
  Pallas kernels  47.2 us (98%)
  between operations  0.64 us (1%)
    pallas_call x1, Pallas kernels, local(): pl.pallas_call(functools.partial(filter_kernel, n_dom, n_rep), out_shape=...  40.8 us
    pallas_call x1, Pallas kernels, local(): pl.pallas_call(functools.partial(solve_kernel, scaling), out_shape=[jax.S...  6.44 us

profile of v2, /device:TPU:1, one launch (start us, length us, event | category | flops | bytes accessed | tf_op | source)
XLA Modules:
  0.0 47.8 jit_solution(13450705709749085544)
XLA Ops:
  0.6 40.8 %filter_and_gram.1 = (f32[128,512]{1,0:T(8,128)S(1)}, f32[32,128]{1,0:T(8,128)S(1)}) custom-call(f32[128,512]{1,0:T(8,128)} %start_hbm.1, f32[8,8,768]{2,1,0:T(8,128)} %maps_hbm.1, s32[1,64]{1,0:T(1,128)} %send_hbm.1, s32[768]{0:T(1024)} %partner_hbm.1), custom_call_target="tpu_custom_call" | custom-call | tf_op jit(solution)/shard_map/filter_and_gram/pallas_call | solution.py:489
  41.4 6.4 %factor_and_solve.1 = (f32[128,512]{1,0:T(8,128)}, f32[64,64]{1,0:T(8,128)}) custom-call(f32[128,512]{1,0:T(8,128)S(1)} %get-tuple-element.4.f_ref, f32[32,128]{1,0:T(8,128)S(1)} %get-tuple-element.5.g_ref), custom_call_target="tpu_custom_call" | custom-call | tf_op jit(solution)/shard_map/factor_and_solve/pallas_call | solution.py:534

commit v3 on v2

--- a/solution.py
+++ b/solution.py
@@ -94,14 +94,6 @@
     base = z * PLANE_DOM
     q = (d - base) * n_rep + r
 
-    def plane_peer(i):
-        t = lax.rem(q + 1 + i, plane)
-        return t, (base + t // n_rep, lax.rem(t, n_rep))
-
-    def z_peer(i):
-        t = lax.rem(z + 1 + i, z_count)
-        return (t * PLANE_DOM + (d - base), r)
-
     up = lax.rem(d + 1, n_dom)
     down = lax.rem(d + n_dom - 1, n_dom)
     nxt = lax.rem(r + 1, n_rep)
@@ -354,27 +346,40 @@
     both = half + pltpu.roll(half, 64, 1)
     lane32 = lax.broadcasted_iota(jnp.int32, (32, 128), 1)
     packed = jnp.where(lane32 < 64, both[0:32, :], both[32:64, :])
-    for i in range(plane):
-        gsl_ref[i] = packed[i : i + 1, :]
+    share = 32 // PLANE_DOM
+    for i in range(PLANE_DOM):
+        gsl_ref[i] = packed[i * share : (i + 1) * share, :]
 
     pl.semaphore_wait(xsem, len(x_peers))
-
-    def reduce_start(i, carry):
-        t, peer = plane_peer(i)
+    chips_x = PLANE_DOM // 2
+    x, c = mine // 2, lax.rem(mine, 2)
+
+    def ring(step, count):
+        return min(step, count - step)
+
+    offsets = [
+        (dx, dy, dc) for dx in range(chips_x) for dy in range(n_rep) for dc in range(2)
+    ][1:]
+    offsets.sort(key=lambda o: -(ring(o[0], chips_x) + ring(o[1], n_rep)))
+
+    def plane_peer(dx, dy, dc):
+        to = lax.rem(x + dx, chips_x) * 2 + lax.rem(c + dc, 2)
+        return to, (base + to, lax.rem(r + dy, n_rep))
+
+    for offset in offsets:
+        to, peer = plane_peer(*offset)
         pltpu.make_async_remote_copy(
-            src_ref=gsl_ref.at[t],
+            src_ref=gsl_ref.at[to],
             dst_ref=rsbuf_ref.at[q],
             send_sem=arsem.at[0],
             recv_sem=arsem.at[1],
             device_id=peer,
             device_id_type=MESH,
         ).start()
-        return carry
-
-    lax.fori_loop(0, plane - 1, reduce_start, 0)
-    rsbuf_ref[q] = gsl_ref[q]
+    rsbuf_ref[q] = gsl_ref[mine]
     for t in range(4):
         f_ref[:, t * 128 : (t + 1) * 128] = vt_ref[t * 128 : (t + 1) * 128, :].T
+    pl.semaphore_wait(zsem.at[1], 2)
     drain(rsbuf_ref, plane - 1, arsem.at[1])
 
     def total(ref, count):
@@ -387,51 +392,79 @@
 
     part_sum = total(rsbuf_ref, plane)
     zsend_ref[0] = part_sum
-    pl.semaphore_wait(zsem.at[1], 2)
-
-    def z_start(i, carry):
+    for by in sorted(range(1, z_count), key=lambda step: -ring(step, z_count)):
         pltpu.make_async_remote_copy(
             src_ref=zsend_ref.at[0],
             dst_ref=zbuf_ref.at[z],
             send_sem=arsem.at[2],
             recv_sem=arsem.at[3],
-            device_id=z_peer(i),
+            device_id=z_shift(by),
             device_id_type=MESH,
         ).start()
-        return carry
-
-    lax.fori_loop(0, z_count - 1, z_start, 0)
     zbuf_ref[z] = part_sum
     drain(zbuf_ref, z_count - 1, arsem.at[3])
     slice_sum = total(zbuf_ref, z_count)
     zsend_ref[1] = slice_sum
-
-    def gather_start(i, carry):
-        pltpu.make_async_remote_copy(
-            src_ref=zsend_ref.at[1],
-            dst_ref=agbuf_ref.at[q],
-            send_sem=arsem.at[4],
-            recv_sem=arsem.at[5],
-            device_id=plane_peer(i)[1],
-            device_id_type=MESH,
-        ).start()
-        return carry
-
-    lax.fori_loop(0, plane - 1, gather_start, 0)
-    agbuf_ref[q] = slice_sum
-    drain(agbuf_ref, plane - 1, arsem.at[5])
-    for i in range(plane):
-        g_ref[i : i + 1, :] = agbuf_ref[i]
+    for offset in offsets:
+        if offset[1] == 0:
+            pltpu.make_async_remote_copy(
+                src_ref=zsend_ref.at[1],
+                dst_ref=agbuf_ref.at[mine],
+                send_sem=arsem.at[4],
+                recv_sem=arsem.at[5],
+                device_id=plane_peer(*offset)[1],
+                device_id_type=MESH,
+            ).start()
+    agbuf_ref[mine] = slice_sum
+    drain(agbuf_ref, PLANE_DOM - 1, arsem.at[5])
+    for i in range(PLANE_DOM):
+        g_ref[i * share : (i + 1) * share, :] = agbuf_ref[i]
 
     for copies in (map_copies, first_copies, second_copies):
         for copy in copies:
             copy.wait_send()
     drain(rsbuf_ref, plane - 1, arsem.at[0])
     drain(zbuf_ref, z_count - 1, arsem.at[2])
-    drain(agbuf_ref, plane - 1, arsem.at[4])
-
-
-def solve_kernel(scaling, f_ref, g_ref, basis_ref, triangle_ref):
+    drain(agbuf_ref, PLANE_DOM - 1, arsem.at[4])
+
+
+def full8(value):
+    return jnp.broadcast_to(value, (8, 128))
+
+
+def eliminate(work):
+    sub = lax.broadcasted_iota(jnp.int32, (8, 128), 0)
+    for g in range(8):
+        cols = [[full8(work[i][:, g * 8 + j : g * 8 + j + 1]) for i in range(g, 8)] for j in range(8)]
+        rows = [full8(work[g][j : j + 1, :]) for j in range(8)]
+        block = [[full8(cols[b][0][a : a + 1, :]) for b in range(a + 1)] for a in range(8)]
+        mult = [[None] * 8 for _ in range(8)]
+        inverse = []
+        for j in range(8):
+            inverse.append(1.0 / block[j][j])
+            for a in range(j + 1, 8):
+                mult[a][j] = block[a][j] * inverse[j]
+            for a in range(j + 1, 8):
+                for b in range(j + 1, a + 1):
+                    block[a][b] = block[a][b] - mult[a][j] * block[b][j]
+                rows[a] = rows[a] - mult[a][j] * rows[j]
+        scaled = [rows[j] * inverse[j] for j in range(8)]
+        done = rows[0]
+        for j in range(1, 8):
+            done = jnp.where(sub == j, rows[j], done)
+        work[g] = done
+        for i in range(g + 1, 8):
+            col = [cols[j][i - g] for j in range(8)]
+            for j in range(8):
+                for t in range(j):
+                    col[j] = col[j] - col[t] * mult[j][t]
+            terms = [col[j] * scaled[j] for j in range(8)]
+            while len(terms) > 1:
+                terms = [terms[t] + terms[t + 1] for t in range(0, len(terms), 2)]
+            work[i] = work[i] - terms[0]
+
+
+def solve_kernel(scaling, f_ref, g_ref, basis_hbm, triangle_ref, basis_ref, sem):
     g = g_ref[...]
     turned = pltpu.roll(g, 64, 1)
     lane32 = lax.broadcasted_iota(jnp.int32, (32, 128), 1)
@@ -441,22 +474,13 @@
     work = [top[i * 8 : (i + 1) * 8, :] for i in range(4)] + [
         bottom[i * 8 : (i + 1) * 8, :] for i in range(4)
     ]
+    eliminate(work)
     sub = lax.broadcasted_iota(jnp.int32, (8, 128), 0)
-    for k in range(COLS):
-        group, row = k // 8, k % 8
-        pivot_row = work[group][row : row + 1, :]
-        scaled = pivot_row / pivot_row[:, k : k + 1]
-        for i in range(group, 8):
-            col = work[i][:, k : k + 1]
-            update = col * scaled
-            if i == group:
-                update = jnp.where(sub > row, update, 0.0)
-            work[i] = work[i] - update
     lane = lax.broadcasted_iota(jnp.int32, (8, 128), 1)
     rows_out = []
     for i in range(8):
         diag = jnp.sum(jnp.where(lane == sub + 8 * i, work[i], 0.0), axis=1, keepdims=True)
-        rows_out.append(work[i] / jnp.sqrt(diag))
+        rows_out.append(work[i] * lax.rsqrt(diag))
     full = jnp.concatenate(rows_out, axis=0)
     lane64 = lax.broadcasted_iota(jnp.int32, (COLS, 128), 1)
     row64 = lax.broadcasted_iota(jnp.int32, (COLS, 128), 0)
@@ -474,12 +498,20 @@
     for t in range(4):
         fhi, flo = split_two(f_ref[:, t * 128 : (t + 1) * 128])
         left = jnp.concatenate([fhi, flo, fhi], axis=1)
-        basis_ref[:, t * 128 : (t + 1) * 128] = dot_nt(left, right)
+        basis_ref[t] = dot_nt(left, right)
+        pltpu.make_async_copy(
+            basis_ref.at[t], basis_hbm.at[:, pl.ds(t * 128, 128)], sem.at[t]
+        ).start()
+    for t in range(4):
+        pltpu.make_async_copy(
+            basis_ref.at[t], basis_hbm.at[:, pl.ds(t * 128, 128)], sem.at[t]
+        ).wait()
 
 
 def local(n_dom, n_rep, start_block, restriction_maps, send_rows, partner):
     z_count = n_dom // PLANE_DOM
     plane = PLANE_DOM * n_rep
+    share = 32 // PLANE_DOM
     vmem = pl.BlockSpec(memory_space=pltpu.VMEM)
     hbm = pl.BlockSpec(memory_space=pltpu.HBM)
     inputs = [
@@ -513,11 +545,11 @@
             pltpu.VMEM((SLOTS, 128), F32),
             pltpu.VMEM((2, SLOTS, WIDE), F32),
             pltpu.VMEM((WIDE, 128), F32),
-            pltpu.VMEM((plane, 1, 128), F32),
-            pltpu.VMEM((plane, 1, 128), F32),
-            pltpu.VMEM((2, 1, 128), F32),
-            pltpu.VMEM((z_count, 1, 128), F32),
-            pltpu.VMEM((plane, 1, 128), F32),
+            pltpu.VMEM((PLANE_DOM, share, 128), F32),
+            pltpu.VMEM((plane, share, 128), F32),
+            pltpu.VMEM((2, share, 128), F32),
+            pltpu.VMEM((z_count, share, 128), F32),
+            pltpu.VMEM((PLANE_DOM, share, 128), F32),
             pltpu.SemaphoreType.DMA((2, 4)),
             pltpu.SemaphoreType.DMA((2, 2, 4)),
             pltpu.SemaphoreType.DMA((6,)),
@@ -538,7 +570,8 @@
             jax.ShapeDtypeStruct((COLS, COLS), F32),
         ],
         in_specs=[vmem, vmem],
-        out_specs=[vmem, vmem],
+        out_specs=[hbm, vmem],
+        scratch_shapes=[pltpu.VMEM((4, NODE_DEV, 128), F32), pltpu.SemaphoreType.DMA((4,))],
         compiler_params=pltpu.CompilerParams(vmem_limit_bytes=16 * 1024 * 1024),
         name="factor_and_solve",
     )(f_rows, gram)

time: 48 us -> 44.2 us (0.921)
  Pallas kernels: 47.2 us -> 43.4 us
    pallas_call x1, Pallas kernels: 6.44 us -> 3.6 us  [local(): pl.pallas_call(functools.partial(solve_kernel, scaling), out_shape=[jax.S...]
    pallas_call x1, Pallas kernels: 40.8 us -> 39.8 us  [local(): pl.pallas_call(functools.partial(filter_kernel, n_dom, n_rep), out_shape=...]
where the time goes in v3:
time: 44.2 us; the launch traced here: 44 us
  Pallas kernels  43.4 us (98%)
  between operations  0.64 us (1%)
    pallas_call x1, Pallas kernels, local(): pl.pallas_call(functools.partial(filter_kernel, n_dom, n_rep), out_shape=...  39.8 us
    pallas_call x1, Pallas kernels, local(): pl.pallas_call(functools.partial(solve_kernel, scaling), out_shape=[jax.S...  3.6 us

profile of v3, /device:TPU:1, one launch (start us, length us, event | category | flops | bytes accessed | tf_op | source)
XLA Modules:
  0.0 44.0 jit_solution(14620172956256122358)
XLA Ops:
  0.6 39.8 %filter_and_gram.1 = (f32[128,512]{1,0:T(8,128)S(1)}, f32[32,128]{1,0:T(8,128)S(1)}) custom-call(f32[128,512]{1,0:T(8,128)} %start_hbm.1, f32[8,8,768]{2,1,0:T(8,128)} %maps_hbm.1, s32[1,64]{1,0:T(1,128)} %send_hbm.1, s32[768]{0:T(1024)} %partner_hbm.1), custom_call_target="tpu_custom_call" | custom-call | tf_op jit(solution)/shard_map/filter_and_gram/pallas_call | solution.py:521
  40.4 3.6 %factor_and_solve.1 = (f32[128,512]{1,0:T(8,128)}, f32[64,64]{1,0:T(8,128)}) custom-call(f32[128,512]{1,0:T(8,128)S(1)} %get-tuple-element.4.f_ref, f32[32,128]{1,0:T(8,128)S(1)} %get-tuple-element.5.g_ref), custom_call_target="tpu_custom_call" | custom-call | tf_op jit(solution)/shard_map/factor_and_solve/pallas_call | solution.py:566

commit v4 on v3

--- a/solution.py
+++ b/solution.py
@@ -111,25 +111,29 @@
             )
         )
     ]
-    for load in loads:
-        load.start()
-
     mine = d - base
     other_core = d + 1 - 2 * lax.rem(d, 2)
     x_peers = [(base + lax.rem(mine + 2 * i, PLANE_DOM), r) for i in range(1, PLANE_DOM // 2)]
     near = [(up, r), (down, r)]
-    near += [(base + lax.rem(mine + i, PLANE_DOM), r) for i in range(1, PLANE_DOM)]
-    for i in range(1, n_rep):
+
+    def z_shift(by):
+        return (lax.rem(z + z_count + by, z_count) * PLANE_DOM + mine, r)
+
+    near += [z_shift(by) for by in (2, -2)]
+    for i in sorted(range(1, n_rep), key=lambda i: -min(i, n_rep - i)):
         turn = lax.rem(r + i, n_rep)
         near += [(d, turn), (other_core, turn)]
-
-    def z_shift(by):
-        return (lax.rem(z + z_count + by, z_count) * PLANE_DOM + mine, r)
-
-    near += [z_shift(by) for by in (1, -1, 2, -2)]
+    near += [
+        (base + lax.rem(mine + i, PLANE_DOM), r)
+        for i in sorted(range(1, PLANE_DOM), key=lambda i: -min(i, PLANE_DOM - i))
+    ]
+    near += [z_shift(by) for by in (1, -1)]
     barrier = pltpu.get_barrier_semaphore()
     for peer in near:
         pl.semaphore_signal(barrier, inc=1, device_id=peer, device_id_type=MESH)
+
+    for load in loads:
+        load.start()
 
     loads[0].wait()
     loads[1].wait()
@@ -164,6 +168,8 @@
     hot = jnp.where(jnp.logical_and(rs[:, 65:66] == lane, used), 1.0, 0.0).astype(BF16)
     hot_wide = jnp.concatenate([hot, hot], axis=1)
     hot_tall = jnp.concatenate([hot, hot], axis=0)
+    same = dot_nt(hot, hot).astype(BF16)
+    same_wide = jnp.concatenate([same, same], axis=1)
 
     sub = lax.broadcasted_iota(jnp.int32, (128, 128), 0).astype(F32)
     rhl = []
@@ -208,7 +214,7 @@
 
     pl.semaphore_wait(barrier, len(near))
     first_copies = value_copies(0)
-    for copy in first_copies + map_copies:
+    for copy in map_copies + first_copies:
         copy.start()
     for peer in x_peers:
         pl.semaphore_signal(xsem, inc=1, device_id=peer, device_id_type=MESH)
@@ -249,9 +255,6 @@
         for copy in copies:
             copy.wait_recv()
 
-    def outgoing(step):
-        vsend_ref[step] = dot_nt(hot_wide, vhl_ref[...])
-
     def local_part(own_ref, out_ref, combine):
         for j in range(3):
             vx_ref[:, j * 256 : (j + 1) * 256] = dot_nn(
@@ -300,10 +303,12 @@
                 cpack_ref[a2 * COLS + cg * 8 : a2 * COLS + cg * 8 + 8, :] = jnp.where(
                     low, hi, acc[a2] - hi
                 )
-        return dot_nn(cpack_ref[...].astype(BF16), hot_tall)
+        return cpack_ref[...].astype(BF16)
 
     spread(vt_ref)
     local_part(vt_ref, t_ref, lambda acc, at: acc)
+    hi, lo = split_two(t_ref[...])
+    vsend_ref[1] = dot_nt(hot_wide, jnp.concatenate([hi, lo], axis=1))
 
     recv_waits(map_copies)
     far_maps = jnp.concatenate([rrecv_ref[...], rrecv_ref[...]], axis=0).T
@@ -316,19 +321,20 @@
             )
         ms_ref[a2 * 8 : (a2 + 1) * 8, :] = acc * (-1.0 / RADIUS)
     recv_waits(first_copies)
-    t_ref[...] = t_ref[...] + remote_part(0)
-
-    spread(t_ref)
-    outgoing(1)
+    packed_far = remote_part(0)
+    vsend_ref[1] = vsend_ref[1] + dot_nt(same_wide, packed_far)
     second_copies = value_copies(1)
     for copy in second_copies:
         copy.start()
+
+    t_ref[...] = t_ref[...] + dot_nn(packed_far, hot_tall)
+    spread(t_ref)
     pl.semaphore_wait(zsem.at[0], 2)
     for by in (4, -4):
         pl.semaphore_signal(zsem.at[1], inc=1, device_id=z_shift(by), device_id_type=MESH)
     local_part(t_ref, vt_ref, lambda acc, at: 2.0 * acc - vt_ref[at, :])
     recv_waits(second_copies)
-    vt_ref[...] = vt_ref[...] + 2.0 * remote_part(1)
+    vt_ref[...] = vt_ref[...] + 2.0 * dot_nn(remote_part(1), hot_tall)
 
     spread(vt_ref)
     tall = jnp.concatenate(

time: 44.2 us -> 44 us (level)
  no operation moved by 1% of the time
where the time goes in v4:
time: 44 us; the launch traced here: 43.8 us
  Pallas kernels  43.2 us (98%)
  between operations  0.64 us (1%)
    pallas_call x1, Pallas kernels, local(): pl.pallas_call(functools.partial(filter_kernel, n_dom, n_rep), out_shape=...  39.6 us
    pallas_call x1, Pallas kernels, local(): pl.pallas_call(functools.partial(solve_kernel, scaling), out_shape=[jax.S...  3.6 us

profile of v4, /device:TPU:1, one launch (start us, length us, event | category | flops | bytes accessed | tf_op | source)
XLA Modules:
  0.0 43.8 jit_solution(6115280630477229949)
XLA Ops:
  0.6 39.6 %filter_and_gram.1 = (f32[128,512]{1,0:T(8,128)S(1)}, f32[32,128]{1,0:T(8,128)S(1)}) custom-call(f32[128,512]{1,0:T(8,128)} %start_hbm.1, f32[8,8,768]{2,1,0:T(8,128)} %maps_hbm.1, s32[1,64]{1,0:T(1,128)} %send_hbm.1, s32[768]{0:T(1024)} %partner_hbm.1), custom_call_target="tpu_custom_call" | custom-call | tf_op jit(solution)/shard_map/filter_and_gram/pallas_call | solution.py:527
  40.2 3.6 %factor_and_solve.1 = (f32[128,512]{1,0:T(8,128)}, f32[64,64]{1,0:T(8,128)}) custom-call(f32[128,512]{1,0:T(8,128)S(1)} %get-tuple-element.4.f_ref, f32[32,128]{1,0:T(8,128)S(1)} %get-tuple-element.5.g_ref), custom_call_target="tpu_custom_call" | custom-call | tf_op jit(solution)/shard_map/factor_and_solve/pallas_call | solution.py:572

commit v5 on v4

--- a/solution.py
+++ b/solution.py
@@ -470,7 +470,9 @@
             work[i] = work[i] - terms[0]
 
 
-def solve_kernel(scaling, f_ref, g_ref, basis_hbm, triangle_ref, basis_ref, sem):
+def solve_kernel(
+    scaling, f_ref, g_ref, basis_hbm, triangle_hbm, basis_ref, triangle_ref, left_ref, sem
+):
     g = g_ref[...]
     turned = pltpu.roll(g, 64, 1)
     lane32 = lax.broadcasted_iota(jnp.int32, (32, 128), 1)
@@ -480,6 +482,10 @@
     work = [top[i * 8 : (i + 1) * 8, :] for i in range(4)] + [
         bottom[i * 8 : (i + 1) * 8, :] for i in range(4)
     ]
+    for t in range(4):
+        fhi, flo = split_two(f_ref[:, t * 128 : (t + 1) * 128])
+        left_ref[t * 128 : (t + 1) * 128, 0:128] = fhi
+        left_ref[t * 128 : (t + 1) * 128, 128:256] = flo
     eliminate(work)
     sub = lax.broadcasted_iota(jnp.int32, (8, 128), 0)
     lane = lax.broadcasted_iota(jnp.int32, (8, 128), 1)
@@ -491,6 +497,8 @@
     lane64 = lax.broadcasted_iota(jnp.int32, (COLS, 128), 1)
     row64 = lax.broadcasted_iota(jnp.int32, (COLS, 128), 0)
     triangle_ref[...] = jnp.where(lane64 >= row64, full * (1.0 / scaling), 0.0)[:, 0:COLS]
+    copies = [pltpu.make_async_copy(triangle_ref, triangle_hbm, sem.at[4])]
+    copies[0].start()
     full = full * scaling
     block = jnp.concatenate(
         [
@@ -500,18 +508,23 @@
         axis=0,
     )
     bhi, blo = split_two(block)
-    right = jnp.concatenate([bhi, bhi, blo], axis=1)
+    right = jnp.concatenate(
+        [
+            jnp.concatenate([bhi, bhi], axis=1),
+            jnp.concatenate([blo, jnp.zeros_like(blo)], axis=1),
+        ],
+        axis=0,
+    )
     for t in range(4):
-        fhi, flo = split_two(f_ref[:, t * 128 : (t + 1) * 128])
-        left = jnp.concatenate([fhi, flo, fhi], axis=1)
-        basis_ref[t] = dot_nt(left, right)
-        pltpu.make_async_copy(
+        both = dot_nt(left_ref[t * 128 : (t + 1) * 128, :], right)
+        basis_ref[t] = both[:, 0:128] + both[:, 128:256]
+        copy = pltpu.make_async_copy(
             basis_ref.at[t], basis_hbm.at[:, pl.ds(t * 128, 128)], sem.at[t]
-        ).start()
-    for t in range(4):
-        pltpu.make_async_copy(
-            basis_ref.at[t], basis_hbm.at[:, pl.ds(t * 128, 128)], sem.at[t]
-        ).wait()
+        )
+        copy.start()
+        copies.append(copy)
+    for copy in copies:
+        copy.wait()
 
 
 def local(n_dom, n_rep, start_block, restriction_maps, send_rows, partner):
@@ -576,8 +589,13 @@
             jax.ShapeDtypeStruct((COLS, COLS), F32),
         ],
         in_specs=[vmem, vmem],
-        out_specs=[hbm, vmem],
-        scratch_shapes=[pltpu.VMEM((4, NODE_DEV, 128), F32), pltpu.SemaphoreType.DMA((4,))],
+        out_specs=[hbm, hbm],
+        scratch_shapes=[
+            pltpu.VMEM((4, NODE_DEV, 128), F32),
+            pltpu.VMEM((COLS, COLS), F32),
+            pltpu.VMEM((4 * NODE_DEV, 256), BF16),
+            pltpu.SemaphoreType.DMA((5,)),
+        ],
         compiler_params=pltpu.CompilerParams(vmem_limit_bytes=16 * 1024 * 1024),
         name="factor_and_solve",
     )(f_rows, gram)

time: 44 us -> 43.4 us (0.986)
  Pallas kernels: 43.2 us -> 42.6 us
    pallas_call x1, Pallas kernels: 3.6 us -> 3.03 us  [local(): pl.pallas_call(functools.partial(solve_kernel, scaling), out_shape=[jax.S...]
where the time goes in v5:
time: 43.4 us; the launch traced here: 43.3 us
  Pallas kernels  42.6 us (98%)
  between operations  0.64 us (1%)
    pallas_call x1, Pallas kernels, local(): pl.pallas_call(functools.partial(filter_kernel, n_dom, n_rep), out_shape=...  39.6 us
    pallas_call x1, Pallas kernels, local(): pl.pallas_call(functools.partial(solve_kernel, scaling), out_shape=[jax.S...  3.03 us

profile of v5, /device:TPU:1, one launch (start us, length us, event | category | flops | bytes accessed | tf_op | source)
XLA Modules:
  0.0 43.3 jit_solution(2052325447088797545)
XLA Ops:
  0.6 39.6 %filter_and_gram.1 = (f32[128,512]{1,0:T(8,128)S(1)}, f32[32,128]{1,0:T(8,128)S(1)}) custom-call(f32[128,512]{1,0:T(8,128)} %start_hbm.1, f32[8,8,768]{2,1,0:T(8,128)} %maps_hbm.1, s32[1,64]{1,0:T(1,128)} %send_hbm.1, s32[768]{0:T(1024)} %partner_hbm.1), custom_call_target="tpu_custom_call" | custom-call | tf_op jit(solution)/shard_map/filter_and_gram/pallas_call | solution.py:540
  40.2 3.0 %factor_and_solve.1 = (f32[128,512]{1,0:T(8,128)}, f32[64,64]{1,0:T(8,128)}) custom-call(f32[128,512]{1,0:T(8,128)S(1)} %get-tuple-element.4.f_ref, f32[32,128]{1,0:T(8,128)S(1)} %get-tuple-element.5.g_ref), custom_call_target="tpu_custom_call" | custom-call | tf_op jit(solution)/shard_map/factor_and_solve/pallas_call | solution.py:585

commit v6 on v5

--- a/solution.py
+++ b/solution.py
@@ -167,8 +167,12 @@
     used = rs[:, 64:65] == expect
     hot = jnp.where(jnp.logical_and(rs[:, 65:66] == lane, used), 1.0, 0.0).astype(BF16)
     hot_wide = jnp.concatenate([hot, hot], axis=1)
-    hot_tall = jnp.concatenate([hot, hot], axis=0)
-    same = dot_nt(hot, hot).astype(BF16)
+    none = jnp.zeros_like(hot)
+    hot_pair = jnp.concatenate(
+        [jnp.concatenate([hot, none], axis=1), jnp.concatenate([none, hot], axis=1)], axis=0
+    )
+    hot_tall = jnp.concatenate([hot_pair, hot_pair], axis=0)
+    same = dot_nt(hot_pair, hot_pair).astype(BF16)
     same_wide = jnp.concatenate([same, same], axis=1)
 
     sub = lax.broadcasted_iota(jnp.int32, (128, 128), 0).astype(F32)
@@ -284,31 +288,59 @@
 
         lax.fori_loop(0, 4, columns, 0)
 
+    half = COLS // 2
+
     def remote_part(step):
-        low = lax.broadcasted_iota(jnp.int32, (8, 128), 1) < SLOTS
-        turned = []
-        for t in range(4):
-            block = vrecv_ref[step, :, t * 128 : (t + 1) * 128]
-            turned.append(jnp.concatenate([block, block], axis=0).T)
-        for cg in range(8):
+        if step == 0:
+            per_tile, stride = 2, COLS
+            pairs = [vrecv_ref[0, :, t * 128 : (t + 1) * 128] for t in range(4)]
+            pairs = [(block, pltpu.roll(block, 128 - half, 1)) for block in pairs]
+        else:
+            per_tile, stride = 4, half
+            pairs = [
+                (
+                    vrecv_ref[1, :, t * 128 : (t + 1) * 128],
+                    vrecv_ref[1, :, 256 + t * 128 : 256 + (t + 1) * 128],
+                )
+                for t in range(2)
+            ]
+        turned = [jnp.concatenate(pair, axis=0).T for pair in pairs]
+        for cg in range(half // 8):
             acc = [jnp.zeros((8, 128), F32) for _ in range(STALK)]
             for b in range(STALK):
-                row = b * COLS + cg * 8
-                val = turned[row // 128][row % 128 : row % 128 + 8, :]
+                row = (b % per_tile) * stride + cg * 8
+                val = turned[b // per_tile][row : row + 8, :]
                 for a2 in range(STALK):
                     coef = row_bcast(ms_ref[a2 * 8 + b : a2 * 8 + b + 1, :])
                     acc[a2] = acc[a2] + coef * val
             for a2 in range(STALK):
+                at = slice(a2 * half + cg * 8, a2 * half + cg * 8 + 8)
                 hi = acc[a2].astype(BF16).astype(F32)
-                cpack_ref[a2 * COLS + cg * 8 : a2 * COLS + cg * 8 + 8, :] = jnp.where(
-                    low, hi, acc[a2] - hi
-                )
+                cpack_ref[at, 0:128] = hi
+                cpack_ref[at, 128:256] = acc[a2] - hi
         return cpack_ref[...].astype(BF16)
+
+    def add_remote(out_ref, packed_slots, scale):
+        sums = dot_nn(packed_slots, hot_tall)
+        for a2 in range(STALK):
+            for h in range(2):
+                at = slice(a2 * COLS + h * half, a2 * COLS + (h + 1) * half)
+                part = sums[a2 * half : (a2 + 1) * half, h * 128 : (h + 1) * 128]
+                out_ref[at, :] = out_ref[at, :] + scale * part
 
     spread(vt_ref)
     local_part(vt_ref, t_ref, lambda acc, at: acc)
     hi, lo = split_two(t_ref[...])
-    vsend_ref[1] = dot_nt(hot_wide, jnp.concatenate([hi, lo], axis=1))
+    both = jnp.concatenate([hi, lo], axis=1)
+    by_half = jnp.concatenate(
+        [
+            both[a * COLS + h * half : a * COLS + (h + 1) * half, :]
+            for h in range(2)
+            for a in range(STALK)
+        ],
+        axis=0,
+    )
+    vsend_ref[1] = dot_nt(hot_wide, by_half)
 
     recv_waits(map_copies)
     far_maps = jnp.concatenate([rrecv_ref[...], rrecv_ref[...]], axis=0).T
@@ -322,19 +354,21 @@
         ms_ref[a2 * 8 : (a2 + 1) * 8, :] = acc * (-1.0 / RADIUS)
     recv_waits(first_copies)
     packed_far = remote_part(0)
-    vsend_ref[1] = vsend_ref[1] + dot_nt(same_wide, packed_far)
+    far_rows = dot_nt(same_wide, packed_far)
+    vsend_ref[1, :, 0:256] = vsend_ref[1, :, 0:256] + far_rows[0:64, :]
+    vsend_ref[1, :, 256:512] = vsend_ref[1, :, 256:512] + far_rows[64:128, :]
     second_copies = value_copies(1)
     for copy in second_copies:
         copy.start()
 
-    t_ref[...] = t_ref[...] + dot_nn(packed_far, hot_tall)
+    add_remote(t_ref, packed_far, 1.0)
     spread(t_ref)
     pl.semaphore_wait(zsem.at[0], 2)
     for by in (4, -4):
         pl.semaphore_signal(zsem.at[1], inc=1, device_id=z_shift(by), device_id_type=MESH)
     local_part(t_ref, vt_ref, lambda acc, at: 2.0 * acc - vt_ref[at, :])
     recv_waits(second_copies)
-    vt_ref[...] = vt_ref[...] + 2.0 * dot_nn(remote_part(1), hot_tall)
+    add_remote(vt_ref, remote_part(1), 2.0)
 
     spread(vt_ref)
     tall = jnp.concatenate(
@@ -348,8 +382,8 @@
         axis=0,
     )
     prod = dot_nt(tall, tall)
-    half = prod[0:64, :] + prod[64:128, :]
-    both = half + pltpu.roll(half, 64, 1)
+    halves = prod[0:64, :] + prod[64:128, :]
+    both = halves + pltpu.roll(halves, 64, 1)
     lane32 = lax.broadcasted_iota(jnp.int32, (32, 128), 1)
     packed = jnp.where(lane32 < 64, both[0:32, :], both[32:64, :])
     share = 32 // PLANE_DOM
@@ -563,7 +597,7 @@
             pltpu.VMEM((2, SLOTS, WIDE), F32),
             pltpu.VMEM((SLOTS, 128), F32),
             pltpu.VMEM((2, SLOTS, WIDE), F32),
-            pltpu.VMEM((WIDE, 128), F32),
+            pltpu.VMEM((WIDE // 2, 256), F32),
             pltpu.VMEM((PLANE_DOM, share, 128), F32),
             pltpu.VMEM((plane, share, 128), F32),
             pltpu.VMEM((2, share, 128), F32),

time: 43.4 us -> 43.3 us (level)
  no operation moved by 1% of the time
where the time goes in v6:
time: 43.3 us; the launch traced here: 43.1 us
  Pallas kernels  42.5 us (98%)
  between operations  0.64 us (1%)
    pallas_call x1, Pallas kernels, local(): pl.pallas_call(functools.partial(filter_kernel, n_dom, n_rep), out_shape=...  39.5 us
    pallas_call x1, Pallas kernels, local(): pl.pallas_call(functools.partial(solve_kernel, scaling), out_shape=[jax.S...  3.02 us

profile of v6, /device:TPU:1, one launch (start us, length us, event | category | flops | bytes accessed | tf_op | source)
XLA Modules:
  0.0 43.1 jit_solution(7650471835384796976)
XLA Ops:
  0.6 39.5 %filter_and_gram.1 = (f32[128,512]{1,0:T(8,128)S(1)}, f32[32,128]{1,0:T(8,128)S(1)}) custom-call(f32[128,512]{1,0:T(8,128)} %start_hbm.1, f32[8,8,768]{2,1,0:T(8,128)} %maps_hbm.1, s32[1,64]{1,0:T(1,128)} %send_hbm.1, s32[768]{0:T(1024)} %partner_hbm.1), custom_call_target="tpu_custom_call" | custom-call | tf_op jit(solution)/shard_map/filter_and_gram/pallas_call | solution.py:574
  40.1 3.0 %factor_and_solve.1 = (f32[128,512]{1,0:T(8,128)}, f32[64,64]{1,0:T(8,128)}) custom-call(f32[128,512]{1,0:T(8,128)S(1)} %get-tuple-element.4.f_ref, f32[32,128]{1,0:T(8,128)S(1)} %get-tuple-element.5.g_ref), custom_call_target="tpu_custom_call" | custom-call | tf_op jit(solution)/shard_map/factor_and_solve/pallas_call | solution.py:619

commit v7 on v6

--- a/solution.py
+++ b/solution.py
@@ -402,9 +402,14 @@
     ][1:]
     offsets.sort(key=lambda o: -(ring(o[0], chips_x) + ring(o[1], n_rep)))
 
+    def slice_of(at_x, at_y, at_c):
+        return lax.rem(at_x + 2 * at_y, chips_x) * 2 + at_c
+
+    my_slice = slice_of(x, r, c)
+
     def plane_peer(dx, dy, dc):
-        to = lax.rem(x + dx, chips_x) * 2 + lax.rem(c + dc, 2)
-        return to, (base + to, lax.rem(r + dy, n_rep))
+        at_x, at_y, at_c = lax.rem(x + dx, chips_x), lax.rem(r + dy, n_rep), lax.rem(c + dc, 2)
+        return slice_of(at_x, at_y, at_c), (base + at_x * 2 + at_c, at_y)
 
     for offset in offsets:
         to, peer = plane_peer(*offset)
@@ -416,7 +421,7 @@
             device_id=peer,
             device_id_type=MESH,
         ).start()
-    rsbuf_ref[q] = gsl_ref[mine]
+    rsbuf_ref[q] = gsl_ref[my_slice]
     for t in range(4):
         f_ref[:, t * 128 : (t + 1) * 128] = vt_ref[t * 128 : (t + 1) * 128, :].T
     pl.semaphore_wait(zsem.at[1], 2)
@@ -445,17 +450,17 @@
     drain(zbuf_ref, z_count - 1, arsem.at[3])
     slice_sum = total(zbuf_ref, z_count)
     zsend_ref[1] = slice_sum
-    for offset in offsets:
-        if offset[1] == 0:
-            pltpu.make_async_remote_copy(
-                src_ref=zsend_ref.at[1],
-                dst_ref=agbuf_ref.at[mine],
-                send_sem=arsem.at[4],
-                recv_sem=arsem.at[5],
-                device_id=plane_peer(*offset)[1],
-                device_id_type=MESH,
-            ).start()
-    agbuf_ref[mine] = slice_sum
+    beside = [(dx, dy, dc) for dx, dy in ((1, 0), (-1, 0), (0, -1)) for dc in range(2)]
+    for dx, dy, dc in beside + [(0, 0, 1)]:
+        pltpu.make_async_remote_copy(
+            src_ref=zsend_ref.at[1],
+            dst_ref=agbuf_ref.at[my_slice],
+            send_sem=arsem.at[4],
+            recv_sem=arsem.at[5],
+            device_id=plane_peer(dx % chips_x, dy % n_rep, dc)[1],
+            device_id_type=MESH,
+        ).start()
+    agbuf_ref[my_slice] = slice_sum
     drain(agbuf_ref, PLANE_DOM - 1, arsem.at[5])
     for i in range(PLANE_DOM):
         g_ref[i * share : (i + 1) * share, :] = agbuf_ref[i]

time: 43.3 us -> 43.1 us (level)
  no operation moved by 1% of the time
where the time goes in v7:
time: 43.1 us; the launch traced here: 43 us
  Pallas kernels  42.3 us (98%)
  between operations  0.64 us (1%)
    pallas_call x1, Pallas kernels, local(): pl.pallas_call(functools.partial(filter_kernel, n_dom, n_rep), out_shape=...  39.3 us
    pallas_call x1, Pallas kernels, local(): pl.pallas_call(functools.partial(solve_kernel, scaling), out_shape=[jax.S...  3.03 us

profile of v7, /device:TPU:1, one launch (start us, length us, event | category | flops | bytes accessed | tf_op | source)
XLA Modules:
  0.0 43.0 jit_solution(2480108248107183)
XLA Ops:
  0.6 39.3 %filter_and_gram.1 = (f32[128,512]{1,0:T(8,128)S(1)}, f32[32,128]{1,0:T(8,128)S(1)}) custom-call(f32[128,512]{1,0:T(8,128)} %start_hbm.1, f32[8,8,768]{2,1,0:T(8,128)} %maps_hbm.1, s32[1,64]{1,0:T(1,128)} %send_hbm.1, s32[768]{0:T(1024)} %partner_hbm.1), custom_call_target="tpu_custom_call" | custom-call | tf_op jit(solution)/shard_map/filter_and_gram/pallas_call | solution.py:579
  39.9 3.0 %factor_and_solve.1 = (f32[128,512]{1,0:T(8,128)}, f32[64,64]{1,0:T(8,128)}) custom-call(f32[128,512]{1,0:T(8,128)S(1)} %get-tuple-element.4.f_ref, f32[32,128]{1,0:T(8,128)S(1)} %get-tuple-element.5.g_ref), custom_call_target="tpu_custom_call" | custom-call | tf_op jit(solution)/shard_map/factor_and_solve/pallas_call | solution.py:624

commit v8 on v7

--- a/solution.py
+++ b/solution.py
@@ -74,6 +74,7 @@
     rrecv_ref,
     vrecv_ref,
     cpack_ref,
+    tall_ref,
     gsl_ref,
     rsbuf_ref,
     zsend_ref,
@@ -368,19 +369,18 @@
         pl.semaphore_signal(zsem.at[1], inc=1, device_id=z_shift(by), device_id_type=MESH)
     local_part(t_ref, vt_ref, lambda acc, at: 2.0 * acc - vt_ref[at, :])
     recv_waits(second_copies)
-    add_remote(vt_ref, remote_part(1), 2.0)
-
-    spread(vt_ref)
-    tall = jnp.concatenate(
-        [
-            jnp.concatenate(
-                [vhl_ref[a * COLS : (a + 1) * COLS, h * 128 : (h + 1) * 128] for a in range(STALK)],
-                axis=1,
-            )
-            for h in range(2)
-        ],
-        axis=0,
-    )
+    far_sums = dot_nn(remote_part(1), hot_tall)
+    for a2 in range(STALK):
+        for h in range(2):
+            at = slice(a2 * COLS + h * half, a2 * COLS + (h + 1) * half)
+            part = far_sums[a2 * half : (a2 + 1) * half, h * 128 : (h + 1) * 128]
+            value = vt_ref[at, :] + 2.0 * part
+            vt_ref[at, :] = value
+            hi, lo = split_two(value)
+            lanes = slice(a2 * 128, (a2 + 1) * 128)
+            tall_ref[h * half : (h + 1) * half, lanes] = hi
+            tall_ref[COLS + h * half : COLS + (h + 1) * half, lanes] = lo
+    tall = tall_ref[...]
     prod = dot_nt(tall, tall)
     halves = prod[0:64, :] + prod[64:128, :]
     both = halves + pltpu.roll(halves, 64, 1)
@@ -479,6 +479,7 @@
 
 def eliminate(work):
     sub = lax.broadcasted_iota(jnp.int32, (8, 128), 0)
+    scales = []
     for g in range(8):
         cols = [[full8(work[i][:, g * 8 + j : g * 8 + j + 1]) for i in range(g, 8)] for j in range(8)]
         rows = [full8(work[g][j : j + 1, :]) for j in range(8)]
@@ -494,10 +495,12 @@
                     block[a][b] = block[a][b] - mult[a][j] * block[b][j]
                 rows[a] = rows[a] - mult[a][j] * rows[j]
         scaled = [rows[j] * inverse[j] for j in range(8)]
-        done = rows[0]
+        done, pivots = rows[0], block[0][0]
         for j in range(1, 8):
             done = jnp.where(sub == j, rows[j], done)
+            pivots = jnp.where(sub == j, block[j][j], pivots)
         work[g] = done
+        scales.append(lax.rsqrt(pivots))
         for i in range(g + 1, 8):
             col = [cols[j][i - g] for j in range(8)]
             for j in range(8):
@@ -507,6 +510,7 @@
             while len(terms) > 1:
                 terms = [terms[t] + terms[t + 1] for t in range(0, len(terms), 2)]
             work[i] = work[i] - terms[0]
+    return scales
 
 
 def solve_kernel(
@@ -525,14 +529,8 @@
         fhi, flo = split_two(f_ref[:, t * 128 : (t + 1) * 128])
         left_ref[t * 128 : (t + 1) * 128, 0:128] = fhi
         left_ref[t * 128 : (t + 1) * 128, 128:256] = flo
-    eliminate(work)
-    sub = lax.broadcasted_iota(jnp.int32, (8, 128), 0)
-    lane = lax.broadcasted_iota(jnp.int32, (8, 128), 1)
-    rows_out = []
-    for i in range(8):
-        diag = jnp.sum(jnp.where(lane == sub + 8 * i, work[i], 0.0), axis=1, keepdims=True)
-        rows_out.append(work[i] * lax.rsqrt(diag))
-    full = jnp.concatenate(rows_out, axis=0)
+    scales = eliminate(work)
+    full = jnp.concatenate([work[i] * scales[i] for i in range(8)], axis=0)
     lane64 = lax.broadcasted_iota(jnp.int32, (COLS, 128), 1)
     row64 = lax.broadcasted_iota(jnp.int32, (COLS, 128), 0)
     triangle_ref[...] = jnp.where(lane64 >= row64, full * (1.0 / scaling), 0.0)[:, 0:COLS]
@@ -603,6 +601,7 @@
             pltpu.VMEM((SLOTS, 128), F32),
             pltpu.VMEM((2, SLOTS, WIDE), F32),
             pltpu.VMEM((WIDE // 2, 256), F32),
+            pltpu.VMEM((2 * COLS, STALK * 128), BF16),
             pltpu.VMEM((PLANE_DOM, share, 128), F32),
             pltpu.VMEM((plane, share, 128), F32),
             pltpu.VMEM((2, share, 128), F32),

time: 43.1 us -> 43 us (level)
  no operation moved by 1% of the time
where the time goes in v8:
time: 43 us; the launch traced here: 42.9 us
  Pallas kernels  42.3 us (98%)
  between operations  0.64 us (1%)
    pallas_call x1, Pallas kernels, local(): pl.pallas_call(functools.partial(filter_kernel, n_dom, n_rep), out_shape=...  39.3 us
    pallas_call x1, Pallas kernels, local(): pl.pallas_call(functools.partial(solve_kernel, scaling), out_shape=[jax.S...  2.95 us

profile of v8, /device:TPU:1, one launch (start us, length us, event | category | flops | bytes accessed | tf_op | source)
XLA Modules:
  0.0 42.9 jit_solution(1591586533664301240)
XLA Ops:
  0.6 39.3 %filter_and_gram.1 = (f32[128,512]{1,0:T(8,128)S(1)}, f32[32,128]{1,0:T(8,128)S(1)}) custom-call(f32[128,512]{1,0:T(8,128)} %start_hbm.1, f32[8,8,768]{2,1,0:T(8,128)} %maps_hbm.1, s32[1,64]{1,0:T(1,128)} %send_hbm.1, s32[768]{0:T(1024)} %partner_hbm.1), custom_call_target="tpu_custom_call" | custom-call | tf_op jit(solution)/shard_map/filter_and_gram/pallas_call | solution.py:577
  40.0 2.9 %factor_and_solve.1 = (f32[128,512]{1,0:T(8,128)}, f32[64,64]{1,0:T(8,128)}) custom-call(f32[128,512]{1,0:T(8,128)S(1)} %get-tuple-element.4.f_ref, f32[32,128]{1,0:T(8,128)S(1)} %get-tuple-element.5.g_ref), custom_call_target="tpu_custom_call" | custom-call | tf_op jit(solution)/shard_map/factor_and_solve/pallas_call | solution.py:623
